TPU v7x, 32 devices: a whole 2x2x4 slice. The times are simulated.
32 devices in a mesh: row: 8 (over y, x, core), col: 4 (over z).
Axes of the slice: x: 2, y: 2, z: 4, core: 2. Of those that a mesh axis runs over, the one named last changes fastest.
Arguments:
- leaf_basis: float32 [64, 64, 256], P(('row', 'col')), may hold values from -0.375 to 0.375
- child_transfer: float32 [64, 4096], P(('row', 'col')), may hold values from -0.5 to 2
- top_transfer: float32 [32, 5, 4096], P(('row', 'col')), may hold values from -0.5 to 2, as said below
- vectors: bfloat16 [16384, 1024], P(('row', 'col')), may hold values from -6 to 6
- near_blocks: bfloat16 [320, 256, 256], P(('row', 'col')), may hold values from -0.375 to 0.375
- near_rows: int32 [320], P(('row', 'col')), may hold values from 0 to 63, as said below
- near_cols: int32 [320], P(('row', 'col')), may hold values from 0 to 63, as said below
- near_counts: int32 [32], P(('row', 'col')), may hold values from 2 to 10, as said below
- coupling: float32 [480, 4096], P(('row', 'col')), may hold values from -0.75 to 0.75
- coupling_rows: int32 [480], P(('row', 'col')), may hold values from 0 to 63, as said below
- coupling_cols: int32 [480], P(('row', 'col')), may hold values from 0 to 63, as said below
- block_counts: int32 [32, 2], P(('row', 'col')), may hold values from 0 to 10, as said below
Outputs:
- ortho_basis: float32 [64, 64, 256], P(('row', 'col'))
- child_new: float32 [64, 4096], P(('row', 'col'))
- top_new: float32 [32, 5, 4096], P(('row', 'col'))
- coupling_new: float32 [480, 4096], P(('row', 'col'))
- product: bfloat16 [16384, 1024], P(('row', 'col'))
Inputs may be any that keep to these rules, and one draw needn't show every extreme that they name: `near_rows`: block i holds rows i * 10 to i * 10 + 9. Its first near_counts[i] slots are live, in no particular order, no pair twice; a live slot's row leaf is one of leaves 2 * i and 2 * i + 1, and its column leaf lies at most 2 leaves from it; every such leaf's pair with itself is live. The other slots hold leaf 2 * i in both entries. `near_cols`: see near_rows. `near_counts`: the bound 10 is reached by some block in every draw. `coupling_rows`: block i holds rows i * 15 to i * 15 + 14: first 10 slots of leaf pairs, then 5 slots of pairs of clusters of level one. In each part the first block_counts[i, level] slots are live, in no particular order, no pair twice; a live slot's row cluster belongs to block i (leaves 2 * i and 2 * i + 1, or cluster i), and its column cluster of the same level lies more than 2 and at most 5 clusters from it. The other slots hold the block's first cluster of that level in both entries. `coupling_cols`: see coupling_rows. `block_counts`: column 0 is at most 10, column 1 at most 5; both bounds are reached by some block in every draw. top_transfer[n, a] is the same for all n with the same n // 2 ** a.
All inputs are finite; a program needn't handle non-finite values.
Results may differ from a plain program's by a relative error of at most 0.0095.
Values may be sent and summed in bfloat16 or wider, within the bound.
A program may use at most 64 MiB of HBM per device.

v0:
```python
import jax
import jax.numpy as jnp
from jax import lax
from jax.sharding import PartitionSpec as P

NEAR_REACH = 2
FAR_MAX = 5
CAND = 5


HIGHEST_PRECISION = lax.Precision.HIGHEST


def swapped(value, axis, stride):
    mask = 2**stride
    pairs = [(source, source ^ mask) for source in range(lax.axis_size(axis))]
    return lax.ppermute(value, axis, pairs)


def shifted(block, axis, distance):
    devices = range(lax.axis_size(axis))
    route = [(i - distance, i) for i in devices if i - distance in devices]
    return lax.ppermute(block, axis, route)


def padded(cells, sides, width):
    for axis, dim in sides:
        count = lax.axis_size(axis)
        ends = count - 1
        head = lax.slice_in_dim(cells, 0, width, axis=dim)
        tail = lax.slice_in_dim(cells, cells.shape[dim] - width, cells.shape[dim], axis=dim)
        cells = jnp.concatenate(
            [
                lax.ppermute(tail, axis, [(i, (i + 1) % count) for i in range(ends)]),
                cells,
                lax.ppermute(head, axis, [((i + 1) % count, i) for i in range(ends)]),
            ],
            axis=dim,
        )
    return cells


def lower_solve(lower_factor, right_side):
    return jax.vmap(
        lambda matrix, column: jax.scipy.linalg.solve_triangular(matrix, column, lower=True)
    )(lower_factor, right_side)


def lift_level(lower_factor, transfer):
    lifted = jnp.einsum("nji,njk->nik", lower_factor, transfer, precision=HIGHEST_PRECISION)
    gram_terms = jnp.einsum("nji,njk->nik", lifted, lifted, precision=HIGHEST_PRECISION)
    return (lifted, gram_terms)


def reproject(lower_factor, lifted):
    return jnp.swapaxes(lower_solve(lower_factor, jnp.swapaxes(lifted, 1, 2)), 1, 2)


def body(
    leaf_basis,
    child_transfer,
    top_transfer,
    vectors,
    near_blocks,
    near_rows,
    near_cols,
    near_counts,
    coupling,
    coupling_rows,
    coupling_cols,
    block_counts,
):
    leaf_count, basis_rank, leaf_points = leaf_basis.shape
    vector_count = vectors.shape[1]
    node_count = leaf_count + 1
    device = lax.axis_index(("row", "col"))
    first_leaf = device * leaf_count
    leaf_gram = jnp.einsum("lkp,ljp->lkj", leaf_basis, leaf_basis, precision=HIGHEST_PRECISION)
    leaf_lower = jnp.linalg.cholesky(leaf_gram)
    ortho_basis = lower_solve(leaf_lower, leaf_basis)
    lifted, gram_terms = lift_level(
        leaf_lower, child_transfer.reshape(leaf_count, basis_rank, basis_rank)
    )
    node_gram = gram_terms[0::2] + gram_terms[1::2]
    node_lower = jnp.linalg.cholesky(node_gram)
    child_new = reproject(jnp.repeat(node_lower, leaf_count, axis=0), lifted)
    lower_now = node_lower
    new_transfers = []
    for level_index in range(lax.axis_size(("row", "col")).bit_length() - 1):
        transfer_now = top_transfer[:, level_index].reshape(1, basis_rank, basis_rank)
        up_lifted, up_term = lift_level(lower_now, transfer_now)
        partner = swapped(up_term, ("row", "col"), level_index)
        lower_now = jnp.linalg.cholesky(up_term + partner)
        new_transfers.append(reproject(lower_now, up_lifted))
    top_new = jnp.concatenate(
        [entry.reshape(1, 1, basis_rank * basis_rank) for entry in new_transfers], axis=1
    )
    send_from = [0 for distance in range(FAR_MAX + 1)]
    factor_stack = jnp.concatenate([leaf_lower, node_lower], axis=0).reshape(
        node_count, basis_rank * basis_rank
    )
    factor_parts = []
    for offset in range(-FAR_MAX, FAR_MAX + 1):
        if offset == 0:
            factor_parts.append(factor_stack)
        else:
            first_node = send_from[abs(offset)]
            arrived = shifted(factor_stack.astype(jnp.bfloat16), ("row", "col"), -offset).astype(
                factor_stack.dtype
            )
            factor_parts.append(
                jnp.concatenate(
                    [jnp.zeros((first_node, basis_rank * basis_rank), jnp.float32), arrived], axis=0
                )
            )
    factor_table = jnp.concatenate(factor_parts, axis=0).reshape(-1, basis_rank, basis_rank)
    slot_index = jnp.arange(coupling.shape[0], dtype=jnp.int32)
    level_split = CAND * leaf_count
    upper_level = slot_index >= level_split
    active = jnp.where(
        upper_level, slot_index - level_split < block_counts[0, 1], slot_index < block_counts[0, 0]
    )
    node_span = jnp.where(upper_level, 1, leaf_count).astype(jnp.int32)
    stack_base = jnp.where(upper_level, leaf_count, 0).astype(jnp.int32)
    row_local = jnp.where(active, coupling_rows - device * node_span + stack_base, stack_base)
    source = coupling_cols // node_span
    position = jnp.where(
        active,
        (source - device + FAR_MAX) * node_count + coupling_cols - source * node_span + stack_base,
        FAR_MAX * node_count + stack_base,
    )
    col_lower = jnp.take(factor_table, position, axis=0)
    row_lower = jnp.take(
        factor_stack.reshape(node_count, basis_rank, basis_rank), row_local, axis=0
    )
    coupling_blocks = coupling.reshape(-1, basis_rank, basis_rank)
    left_half = jnp.einsum("bji,bjk->bik", row_lower, coupling_blocks, precision=HIGHEST_PRECISION)
    recompressed = jnp.einsum("bik,bkj->bij", left_half, col_lower, precision=HIGHEST_PRECISION)
    recompressed = jnp.where(active[:, None, None], recompressed, 0.0)
    ortho_low = ortho_basis.astype(jnp.bfloat16)
    leaf_vectors = vectors.reshape(leaf_count, leaf_points, vector_count)
    leaf_coeff = jnp.einsum(
        "lkp,lpv->lkv", ortho_low, leaf_vectors, preferred_element_type=jnp.float32
    )
    node_coeff = jnp.einsum("lij,liv->jv", child_new, leaf_coeff, precision=HIGHEST_PRECISION)
    coeff_stack = jnp.concatenate([leaf_coeff, node_coeff[None]], axis=0).astype(jnp.bfloat16)
    coeff_parts = []
    for offset in range(-FAR_MAX, FAR_MAX + 1):
        if offset == 0:
            coeff_parts.append(coeff_stack)
        else:
            first_node = send_from[abs(offset)]
            arrived = shifted(coeff_stack, ("row", "col"), -offset)
            coeff_parts.append(
                jnp.concatenate(
                    [jnp.zeros((first_node, basis_rank, vector_count), jnp.bfloat16), arrived],
                    axis=0,
                )
            )
    coeff_table = jnp.concatenate(coeff_parts, axis=0)
    coupling_low = recompressed.astype(jnp.bfloat16)
    gathered = jnp.take(coeff_table, position, axis=0)
    far_terms = jnp.einsum(
        "bij,bjv->biv", coupling_low, gathered, preferred_element_type=jnp.float32
    )
    row_onehot = (row_local[:, None] == jnp.arange(node_count, dtype=jnp.int32)[None, :]).astype(
        jnp.float32
    )
    collected = jnp.einsum("bn,biv->niv", row_onehot, far_terms, precision=HIGHEST_PRECISION)
    descended = (
        collected[:leaf_count]
        + jnp.einsum("lij,jv->liv", child_new, collected[leaf_count], precision=HIGHEST_PRECISION)
    ).astype(jnp.bfloat16)
    far_part = jnp.einsum("lkp,lkv->lpv", ortho_low, descended, preferred_element_type=jnp.float32)
    extended = padded(vectors, ((("row", "col"), 0),), NEAR_REACH * leaf_points)
    window = extended.reshape(leaf_count + 2 * NEAR_REACH, leaf_points, vector_count)
    near_slots = near_rows.shape[0]
    near_active = jnp.arange(near_slots, dtype=jnp.int32) < near_counts[0]
    near_row = jnp.where(near_active, near_rows - first_leaf, 0)
    near_col = jnp.where(near_active, near_cols - first_leaf + NEAR_REACH, NEAR_REACH)

    def accumulate(block_index, running):
        source_rows = lax.dynamic_index_in_dim(window, near_col[block_index], 0, keepdims=False)
        block_product = jnp.dot(
            near_blocks[block_index], source_rows, preferred_element_type=jnp.float32
        )
        block_product = jnp.where(near_active[block_index], block_product, 0.0)
        target = near_row[block_index]
        current = lax.dynamic_index_in_dim(running, target, 0, keepdims=False)
        return lax.dynamic_update_index_in_dim(running, current + block_product, target, 0)

    near_sum = lax.fori_loop(
        0, near_slots, accumulate, jnp.zeros((leaf_count, leaf_points, vector_count), jnp.float32)
    )
    product = (
        (near_sum + far_part).astype(jnp.bfloat16).reshape(leaf_count * leaf_points, vector_count)
    )
    return (
        ortho_basis,
        child_new.reshape(leaf_count, basis_rank * basis_rank),
        top_new,
        recompressed.reshape(-1, basis_rank * basis_rank),
        product,
    )


def solution(mesh):
    in_specs = (
        P(("row", "col"), None, None),
        P(("row", "col"), None),
        P(("row", "col"), None, None),
        P(("row", "col"), None),
        P(("row", "col"), None, None),
        P(("row", "col")),
        P(("row", "col")),
        P(("row", "col")),
        P(("row", "col"), None),
        P(("row", "col")),
        P(("row", "col")),
        P(("row", "col"), None),
    )
    out_specs = (
        P(("row", "col"), None, None),
        P(("row", "col"), None),
        P(("row", "col"), None, None),
        P(("row", "col"), None),
        P(("row", "col"), None),
    )
    return jax.shard_map(body, mesh=mesh, in_specs=in_specs, out_specs=out_specs, check_vma=False)
```

profile of v0, /device:TPU:0, one launch (start us, length us, event | category | flops | bytes accessed | tf_op | source)
XLA Modules:
  0.0 397.3 jit_solution(11288508503294884119)
XLA Ops:
  1.9 11.7 %custom-call.18 = f32[2,64,64]{2,1,0:T(8,128)S(1)} custom-call(f32[2,64,64]{2,1,0:T(8,128)S(1)} %fusion.31), custom_call_target="Cholesky" | custom-call | tf_op jit(solution)/shard_map/jit(cholesky)/cholesky | solution.py:79
  15.4 5.8 %custom-call.30 = f32[1,64,64]{2,1,0:T(8,128)S(1)} custom-call(f32[1,64,64]{2,1,0:T(8,128)S(1)} %fusion.56), custom_call_target="Cholesky" | custom-call | tf_op jit(solution)/shard_map/jit(cholesky)/cholesky | solution.py:85
  22.7 9.8 %custom-call.20 = f32[2,1,64,64]{2,3,1,0:T(8,128)S(1)} custom-call(f32[2,1,64,64]{3,2,1,0:T(8,128)S(1)} %broadcast_select_fusion), custom_call_target="InvertDiagBlocksLowerTriangular" | custom-call | tf_op jit(solution)/shard_map/vmap(jit(_solve_triangular))/triangular_solve | solution.py:45
  32.7 9.8 %custom-call.19 = f32[2,1,64,64]{2,3,1,0:T(8,128)S(1)} custom-call(f32[2,1,64,64]{3,2,1,0:T(8,128)S(1)} %get-tuple-element.171), custom_call_target="InvertDiagBlocksLowerTriangular" | custom-call | tf_op jit(solution)/shard_map/vmap(jit(_solve_triangular))/triangular_solve | solution.py:45
  42.9 1.6 fusion.93
  45.8 5.3 %collective-permute-start.17 = (bf16[3,64,1024]{2,1,0:T(8,128)(2,1)}, bf16[3,64,1024]{2,1,0:T(8,128)(2,1)}, u32[]{:S(2)}, u32[]{:S(2)}) collective-permute-start(bf16[3,64,1024]{2,1,0:T(8,128)(2,1)} %pad_maximum_fusion.1), channel_id=1, source_target_pairs={{0,5},{1,6},{2,7},{3,8},{4,9},{5,10},{6,11},{7,12},{8,13},{9,14},{... | collective-permute-start | bytes 1179656 | tf_op jit(solution)/shard_map/ppermute | solution.py:23
  51.0 4.3 %collective-permute-start.18 = (bf16[3,64,1024]{2,1,0:T(8,128)(2,1)}, bf16[3,64,1024]{2,1,0:T(8,128)(2,1)}, u32[]{:S(2)}, u32[]{:S(2)}) collective-permute-start(bf16[3,64,1024]{2,1,0:T(8,128)(2,1)} %pad_maximum_fusion.1), channel_id=1, source_target_pairs={{0,4},{1,5},{2,6},{3,7},{4,8},{5,9},{6,10},{7,11},{8,12},{9,13},{1... | collective-permute-start | bytes 1179656 | tf_op jit(solution)/shard_map/ppermute | solution.py:23
  55.3 4.2 %collective-permute-start.19 = (bf16[3,64,1024]{2,1,0:T(8,128)(2,1)}, bf16[3,64,1024]{2,1,0:T(8,128)(2,1)}, u32[]{:S(2)}, u32[]{:S(2)}) collective-permute-start(bf16[3,64,1024]{2,1,0:T(8,128)(2,1)} %pad_maximum_fusion.1), channel_id=1, source_target_pairs={{0,3},{1,4},{2,5},{3,6},{4,7},{5,8},{6,9},{7,10},{8,11},{9,12},{10... | collective-permute-start | bytes 1179656 | tf_op jit(solution)/shard_map/ppermute | solution.py:23
  59.5 2.3 collective-permute-start.20
  64.7 1.4 compare_and_fusion
  69.9 7.7 %collective-permute-done = f32[1,64,64]{1,2,0:T(8,128)S(1)} collective-permute-done((f32[1,64,64]{1,2,0:T(8,128)S(1)}, f32[1,64,64]{1,2,0:T(8,128)S(1)}, u32[]{:S(2)}, u32[]{:S(2)}) %collective-permute-start) | collective-permute-done | bytes 16416 | tf_op jit(solution)/shard_map/ppermute | solution.py:17
  77.5 4.0 %collective-permute-start.5 = (bf16[3,4096]{1,0:T(4,128)(2,1)S(1)}, bf16[3,4096]{1,0:T(4,128)(2,1)S(1)}, u32[]{:S(2)}, u32[]{:S(2)}) collective-permute-start(bf16[3,4096]{1,0:T(4,128)(2,1)S(1)} %convert_element_type.14), channel_id=1, source_target_pairs={{0,5},{1,6},{2,7},{3,8},{4,9},{5,10},{6,11},{7,12},{8,13},{9,14},{... | collective-permute-start | bytes 73736 | tf_op jit(solution)/shard_map/ppermute | solution.py:23
  81.7 5.8 %custom-call.31 = f32[1,64,64]{2,1,0:T(8,128)S(1)} custom-call(f32[1,64,64]{2,1,0:T(8,128)S(1)} %fusion.55), custom_call_target="Cholesky" | custom-call | tf_op jit(solution)/shard_map/jit(cholesky)/cholesky | solution.py:93
  90.0 4.9 %custom-call.32 = f32[1,1,64,64]{2,3,1,0:T(8,128)S(1)} custom-call(f32[1,1,64,64]{3,2,1,0:T(8,128)S(1)} %select_bitcast_fusion.4), custom_call_target="InvertDiagBlocksLowerTriangular" | custom-call | tf_op jit(solution)/shard_map/vmap(jit(_solve_triangular))/triangular_solve | solution.py:45
  95.3 2.6 collective-permute-start.6
  98.7 3.7 collective-permute-start.7
  104.1 4.0 collective-permute-start.8
  109.6 4.7 %collective-permute-start.9 = (bf16[3,4096]{1,0:T(4,128)(2,1)S(1)}, bf16[3,4096]{1,0:T(4,128)(2,1)S(1)}, u32[]{:S(2)}, u32[]{:S(2)}) collective-permute-start(bf16[3,4096]{1,0:T(4,128)(2,1)S(1)} %convert_element_type.14), channel_id=1, source_target_pairs={{0,1},{1,2},{2,3},{3,4},{4,5},{5,6},{6,7},{7,8},{8,9},{9,10},{10,1... | collective-permute-start | bytes 73736 | tf_op jit(solution)/shard_map/ppermute | solution.py:23
  119.8 2.2 collective-permute-done.10
  124.0 5.1 %collective-permute-done.11 = bf16[3,4096]{1,0:T(4,128)(2,1)S(1)} collective-permute-done((bf16[3,4096]{1,0:T(4,128)(2,1)S(1)}, bf16[3,4096]{1,0:T(4,128)(2,1)S(1)}, u32[]{:S(2)}, u32[]{:S(2)}) %collective-permute-start.11) | collective-permute-done | bytes 24608 | tf_op jit(solution)/shard_map/ppermute | solution.py:23
  131.1 6.7 %collective-permute-done.12 = bf16[3,4096]{1,0:T(4,128)(2,1)S(1)} collective-permute-done((bf16[3,4096]{1,0:T(4,128)(2,1)S(1)}, bf16[3,4096]{1,0:T(4,128)(2,1)S(1)}, u32[]{:S(2)}, u32[]{:S(2)}) %collective-permute-start.12) | collective-permute-done | bytes 24608 | tf_op jit(solution)/shard_map/ppermute | solution.py:23
  139.8 2.5 collective-permute-done.13
  142.3 1.5 collective-permute-start.14
  144.5 4.9 %collective-permute-done.14 = bf16[3,4096]{1,0:T(4,128)(2,1)S(1)} collective-permute-done((bf16[3,4096]{1,0:T(4,128)(2,1)S(1)}, bf16[3,4096]{1,0:T(4,128)(2,1)S(1)}, u32[]{:S(2)}, u32[]{:S(2)}) %collective-permute-start.14) | collective-permute-done | bytes 24608 | tf_op jit(solution)/shard_map/ppermute | solution.py:23
  149.4 2.6 collective-permute-start.1
  152.7 1.8 gather_fusion.1
  156.2 5.8 %custom-call.33 = f32[1,64,64]{2,1,0:T(8,128)S(1)} custom-call(f32[1,64,64]{2,1,0:T(8,128)S(1)} %fusion.51), custom_call_target="Cholesky" | custom-call | tf_op jit(solution)/shard_map/jit(cholesky)/cholesky | solution.py:93
  164.5 4.5 %collective-permute-start.2 = (f32[1,64,64]{1,2,0:T(8,128)S(1)}, f32[1,64,64]{1,2,0:T(8,128)S(1)}, u32[]{:S(2)}, u32[]{:S(2)}) collective-permute-start(f32[1,64,64]{1,2,0:T(8,128)S(1)} %convolution_bitcast_fusion.6), channel_id=1, source_target_pairs={{0,4},{1,5},{2,6},{3,7},{4,0},{5,1},{6,2},{7,3},{8,12},{9,13},{10,... | collective-permute-start | bytes 49160 | tf_op jit(solution)/shard_map/ppermute | solution.py:17
  169.0 4.9 %custom-call.34 = f32[1,1,64,64]{2,3,1,0:T(8,128)S(1)} custom-call(f32[1,1,64,64]{3,2,1,0:T(8,128)S(1)} %select_bitcast_fusion.3), custom_call_target="InvertDiagBlocksLowerTriangular" | custom-call | tf_op jit(solution)/shard_map/vmap(jit(_solve_triangular))/triangular_solve | solution.py:45
  174.5 5.8 %custom-call.35 = f32[1,64,64]{2,1,0:T(8,128)S(1)} custom-call(f32[1,64,64]{2,1,0:T(8,128)S(1)} %fusion.47), custom_call_target="Cholesky" | custom-call | tf_op jit(solution)/shard_map/jit(cholesky)/cholesky | solution.py:93
  182.8 3.9 collective-permute-start.3
  186.7 4.9 %custom-call.36 = f32[1,1,64,64]{2,3,1,0:T(8,128)S(1)} custom-call(f32[1,1,64,64]{3,2,1,0:T(8,128)S(1)} %select_bitcast_fusion.2), custom_call_target="InvertDiagBlocksLowerTriangular" | custom-call | tf_op jit(solution)/shard_map/vmap(jit(_solve_triangular))/triangular_solve | solution.py:45
  192.1 5.8 %custom-call.37 = f32[1,64,64]{2,1,0:T(8,128)S(1)} custom-call(f32[1,64,64]{2,1,0:T(8,128)S(1)} %fusion.43), custom_call_target="Cholesky" | custom-call | tf_op jit(solution)/shard_map/jit(cholesky)/cholesky | solution.py:93
  200.7 4.9 %custom-call.38 = f32[1,1,64,64]{2,3,1,0:T(8,128)S(1)} custom-call(f32[1,1,64,64]{3,2,1,0:T(8,128)S(1)} %select_bitcast_fusion.1), custom_call_target="InvertDiagBlocksLowerTriangular" | custom-call | tf_op jit(solution)/shard_map/vmap(jit(_solve_triangular))/triangular_solve | solution.py:45
  206.0 6.7 %collective-permute-start.21 = (bf16[3,64,1024]{2,1,0:T(8,128)(2,1)}, bf16[3,64,1024]{2,1,0:T(8,128)(2,1)S(1)}, u32[]{:S(2)}, u32[]{:S(2)}) collective-permute-start(bf16[3,64,1024]{2,1,0:T(8,128)(2,1)} %pad_maximum_fusion.1), channel_id=1, source_target_pairs={{0,1},{1,2},{2,3},{3,4},{4,5},{5,6},{6,7},{7,8},{8,9},{9,10},{10,1... | collective-permute-start | bytes 1179656 | tf_op jit(solution)/shard_map/ppermute | solution.py:23
  212.9 5.8 %custom-call.39 = f32[1,64,64]{2,1,0:T(8,128)S(1)} custom-call(f32[1,64,64]{2,1,0:T(8,128)S(1)} %fusion.39), custom_call_target="Cholesky" | custom-call | tf_op jit(solution)/shard_map/jit(cholesky)/cholesky | solution.py:93
  220.1 4.9 %custom-call.40 = f32[1,1,64,64]{2,3,1,0:T(8,128)S(1)} custom-call(f32[1,1,64,64]{3,2,1,0:T(8,128)S(1)} %fusion.32), custom_call_target="InvertDiagBlocksLowerTriangular" | custom-call | tf_op jit(solution)/shard_map/vmap(jit(_solve_triangular))/triangular_solve | solution.py:45
  226.3 1.3 collective-permute-start.22
  227.5 1.8 constant_dynamic-update-slice_fusion.23
  229.3 1.3 collective-permute-start.23
  230.6 1.8 constant_dynamic-update-slice_fusion.22
  232.4 1.3 collective-permute-start.24
  233.7 1.8 constant_dynamic-update-slice_fusion.21
  236.7 1.8 constant_dynamic-update-slice_fusion.20
  241.9 17.9 %collective-permute-start.15 = (bf16[512,1024]{1,0:T(8,128)(2,1)}, bf16[512,1024]{1,0:T(8,128)(2,1)}, u32[]{:S(2)}, u32[]{:S(2)}) collective-permute-start(bf16[512,1024]{1,0:T(8,128)(2,1)} %param.20), channel_id=1, source_target_pairs={{0,1},{1,2},{2,3},{3,4},{4,5},{5,6},{6,7},{7,8},{8,9},{9,10},{10,1... | collective-permute-start | bytes 3145736 | tf_op jit(solution)/shard_map/ppermute | solution.py:34
  260.6 27.0 %collective-permute-done.23 = bf16[3,64,1024]{2,1,0:T(8,128)(2,1)S(1)} collective-permute-done((bf16[3,64,1024]{2,1,0:T(8,128)(2,1)}, bf16[3,64,1024]{2,1,0:T(8,128)(2,1)S(1)}, u32[]{:S(2)}, u32[]{:S(2)}) %collective-permute-start.23) | collective-permute-done | bytes 393248 | tf_op jit(solution)/shard_map/ppermute | solution.py:23
  287.6 1.5 collective-permute-start.16
  292.2 2.9 gather_fusion.2
  295.8 3.7 fusion.8
  300.7 1.8 fusion.57
  302.6 9.8 %collective-permute-done.16 = bf16[512,1024]{1,0:T(8,128)(2,1)} collective-permute-done((bf16[512,1024]{1,0:T(8,128)(2,1)}, bf16[512,1024]{1,0:T(8,128)(2,1)}, u32[]{:S(2)}, u32[]{:S(2)}) %collective-permute-start.16) | collective-permute-done | bytes 1048608 | tf_op jit(solution)/shard_map/ppermute | solution.py:36
  312.4 3.2 pad_maximum_fusion
  315.9 78.6 %while.13 = (s32[]{:T(128)}, f32[2,256,1024]{2,1,0:T(8,128)S(1)}, s32[10]{0:T(128)S(1)}, pred[10]{0:T(512)(128)(4,1)S(1)}, bf16[10,256,256]{2,1,0:T(8,128)(2,1)}...) while((s32[]{:T(128)}, f32[2,256,1024]{2,1,0:T(8,128)S(1)}, ...), condition=%wide.region_5.8_spmd, body=%wide.region_4.7_spmd.sunk | while | flops 134742016 | bytes 4850907 | solution.py:192
  321.7 2.1 fusion.133
  329.5 2.1 fusion.133
  337.4 2.1 fusion.133
  345.2 2.1 fusion.133
  353.1 2.1 fusion.133
  361.0 2.1 fusion.133
  368.8 2.1 fusion.133
  376.7 2.1 fusion.133
  384.5 2.1 fusion.133
  392.4 2.1 fusion.133
  394.5 2.9 add_convert_fusion
  (222 shorter events, 74.6 us)
Async XLA Ops:
  0.6 0.9 copy-start
  22.6 39.8 %copy-start.3 = (f32[1,5,4096]{2,0,1:T(1,128)S(1)}, f32[1,5,4096]{2,0,1:T(1,128)}, u32[]{:S(2)}) copy-start(f32[1,5,4096]{2,0,1:T(1,128)} %param.19) | copy-start | bytes 245764
  42.9 257.9 %copy-start.1 = (f32[2,64,256]{2,1,0:T(8,128)}, f32[2,64,256]{2,1,0:T(8,128)S(1)}, u32[]{:S(2)}) copy-start(f32[2,64,256]{2,1,0:T(8,128)S(1)} %fusion.29) | copy-start | bytes 393220
  42.9 21.2 %copy-start.4 = (s32[1,2]{1,0:T(1,128)S(1)}, s32[1,2]{1,0:T(1,128)}, u32[]{:S(2)}) copy-start(s32[1,2]{1,0:T(1,128)} %param.28) | copy-start | bytes 28
  42.9 21.8 %copy-start.5 = (s32[15]{0:T(128)S(1)}, s32[15]{0:T(128)}, u32[]{:S(2)}) copy-start(s32[15]{0:T(128)} %param.27) | copy-start | bytes 184
  42.9 23.3 %copy-start.6 = (s32[15]{0:T(128)S(1)}, s32[15]{0:T(128)}, u32[]{:S(2)}) copy-start(s32[15]{0:T(128)} %param.26) | copy-start | bytes 184
  42.9 23.3 %copy-start.2 = (f32[15,4096]{1,0:T(8,128)S(1)}, f32[15,4096]{1,0:T(8,128)}, u32[]{:S(2)}) copy-start(f32[15,4096]{1,0:T(8,128)} %param.25) | copy-start | bytes 737284
  45.7 23.0 %copy-start.7 = (s32[10]{0:T(128)S(1)}, s32[10]{0:T(128)}, u32[]{:S(2)}) copy-start(s32[10]{0:T(128)} %param.23) | copy-start | bytes 124
  45.7 23.0 %copy-start.8 = (s32[10]{0:T(128)S(1)}, s32[10]{0:T(128)}, u32[]{:S(2)}) copy-start(s32[10]{0:T(128)} %param.22) | copy-start | bytes 124
  45.8 180.5 %collective-permute-start.17 = (bf16[3,64,1024]{2,1,0:T(8,128)(2,1)}, bf16[3,64,1024]{2,1,0:T(8,128)(2,1)}, u32[]{:S(2)}, u32[]{:S(2)}) collective-permute-start(bf16[3,64,1024]{2,1,0:T(8,128)(2,1)} %pad_maximum_fusion.1), channel_id=1, source_target_pairs={{0,5},{1,6},{2,7},{3,8},{4,9},{5,10},{6,11},{7,12},{8,13},{9,14},{... | collective-permute-start | bytes 1179656 | tf_op jit(solution)/shard_map/ppermute | solution.py:23
  51.0 178.3 %collective-permute-start.18 = (bf16[3,64,1024]{2,1,0:T(8,128)(2,1)}, bf16[3,64,1024]{2,1,0:T(8,128)(2,1)}, u32[]{:S(2)}, u32[]{:S(2)}) collective-permute-start(bf16[3,64,1024]{2,1,0:T(8,128)(2,1)} %pad_maximum_fusion.1), channel_id=1, source_target_pairs={{0,4},{1,5},{2,6},{3,7},{4,8},{5,9},{6,10},{7,11},{8,12},{9,13},{1... | collective-permute-start | bytes 1179656 | tf_op jit(solution)/shard_map/ppermute | solution.py:23
  55.3 177.1 %collective-permute-start.19 = (bf16[3,64,1024]{2,1,0:T(8,128)(2,1)}, bf16[3,64,1024]{2,1,0:T(8,128)(2,1)}, u32[]{:S(2)}, u32[]{:S(2)}) collective-permute-start(bf16[3,64,1024]{2,1,0:T(8,128)(2,1)} %pad_maximum_fusion.1), channel_id=1, source_target_pairs={{0,3},{1,4},{2,5},{3,6},{4,7},{5,8},{6,9},{7,10},{8,11},{9,12},{10... | collective-permute-start | bytes 1179656 | tf_op jit(solution)/shard_map/ppermute | solution.py:23
  59.5 176.0 %collective-permute-start.20 = (bf16[3,64,1024]{2,1,0:T(8,128)(2,1)}, bf16[3,64,1024]{2,1,0:T(8,128)(2,1)}, u32[]{:S(2)}, u32[]{:S(2)}) collective-permute-start(bf16[3,64,1024]{2,1,0:T(8,128)(2,1)} %pad_maximum_fusion.1), channel_id=1, source_target_pairs={{0,2},{1,3},{2,4},{3,5},{4,6},{5,7},{6,8},{7,9},{8,10},{9,11},{10,... | collective-permute-start | bytes 1179656 | tf_op jit(solution)/shard_map/ppermute | solution.py:23
  63.3 14.3 %collective-permute-start = (f32[1,64,64]{1,2,0:T(8,128)S(1)}, f32[1,64,64]{1,2,0:T(8,128)S(1)}, u32[]{:S(2)}, u32[]{:S(2)}) collective-permute-start(f32[1,64,64]{1,2,0:T(8,128)S(1)} %convolution_bitcast_fusion.10), channel_id=1, source_target_pairs={{0,1},{1,0},{2,3},{3,2},{4,5},{5,4},{6,7},{7,6},{8,9},{9,8},{10,11... | collective-permute-start | bytes 49160 | tf_op jit(solution)/shard_map/ppermute | solution.py:17
  77.5 17.8 %collective-permute-start.5 = (bf16[3,4096]{1,0:T(4,128)(2,1)S(1)}, bf16[3,4096]{1,0:T(4,128)(2,1)S(1)}, u32[]{:S(2)}, u32[]{:S(2)}) collective-permute-start(bf16[3,4096]{1,0:T(4,128)(2,1)S(1)} %convert_element_type.14), channel_id=1, source_target_pairs={{0,5},{1,6},{2,7},{3,8},{4,9},{5,10},{6,11},{7,12},{8,13},{9,14},{... | collective-permute-start | bytes 73736 | tf_op jit(solution)/shard_map/ppermute | solution.py:23
  95.3 3.4 collective-permute-start.6
  98.7 5.3 %collective-permute-start.7 = (bf16[3,4096]{1,0:T(4,128)(2,1)S(1)}, bf16[3,4096]{1,0:T(4,128)(2,1)S(1)}, u32[]{:S(2)}, u32[]{:S(2)}) collective-permute-start(bf16[3,4096]{1,0:T(4,128)(2,1)S(1)} %convert_element_type.14), channel_id=1, source_target_pairs={{0,3},{1,4},{2,5},{3,6},{4,7},{5,8},{6,9},{7,10},{8,11},{9,12},{10... | collective-permute-start | bytes 73736 | tf_op jit(solution)/shard_map/ppermute | solution.py:23
  104.1 5.6 %collective-permute-start.8 = (bf16[3,4096]{1,0:T(4,128)(2,1)S(1)}, bf16[3,4096]{1,0:T(4,128)(2,1)S(1)}, u32[]{:S(2)}, u32[]{:S(2)}) collective-permute-start(bf16[3,4096]{1,0:T(4,128)(2,1)S(1)} %convert_element_type.14), channel_id=1, source_target_pairs={{0,2},{1,3},{2,4},{3,5},{4,6},{5,7},{6,8},{7,9},{8,10},{9,11},{10,... | collective-permute-start | bytes 73736 | tf_op jit(solution)/shard_map/ppermute | solution.py:23
  109.6 6.2 %collective-permute-start.9 = (bf16[3,4096]{1,0:T(4,128)(2,1)S(1)}, bf16[3,4096]{1,0:T(4,128)(2,1)S(1)}, u32[]{:S(2)}, u32[]{:S(2)}) collective-permute-start(bf16[3,4096]{1,0:T(4,128)(2,1)S(1)} %convert_element_type.14), channel_id=1, source_target_pairs={{0,1},{1,2},{2,3},{3,4},{4,5},{5,6},{6,7},{7,8},{8,9},{9,10},{10,1... | collective-permute-start | bytes 73736 | tf_op jit(solution)/shard_map/ppermute | solution.py:23
  115.9 6.1 %collective-permute-start.10 = (bf16[3,4096]{1,0:T(4,128)(2,1)S(1)}, bf16[3,4096]{1,0:T(4,128)(2,1)S(1)}, u32[]{:S(2)}, u32[]{:S(2)}) collective-permute-start(bf16[3,4096]{1,0:T(4,128)(2,1)S(1)} %convert_element_type.14), channel_id=1, source_target_pairs={{1,0},{2,1},{3,2},{4,3},{5,4},{6,5},{7,6},{8,7},{9,8},{10,9},{11,1... | collective-permute-start | bytes 73736 | tf_op jit(solution)/shard_map/ppermute | solution.py:23
  122.0 7.1 %collective-permute-start.11 = (bf16[3,4096]{1,0:T(4,128)(2,1)S(1)}, bf16[3,4096]{1,0:T(4,128)(2,1)S(1)}, u32[]{:S(2)}, u32[]{:S(2)}) collective-permute-start(bf16[3,4096]{1,0:T(4,128)(2,1)S(1)} %convert_element_type.14), channel_id=1, source_target_pairs={{2,0},{3,1},{4,2},{5,3},{6,4},{7,5},{8,6},{9,7},{10,8},{11,9},{12,... | collective-permute-start | bytes 73736 | tf_op jit(solution)/shard_map/ppermute | solution.py:23
  129.1 8.7 %collective-permute-start.12 = (bf16[3,4096]{1,0:T(4,128)(2,1)S(1)}, bf16[3,4096]{1,0:T(4,128)(2,1)S(1)}, u32[]{:S(2)}, u32[]{:S(2)}) collective-permute-start(bf16[3,4096]{1,0:T(4,128)(2,1)S(1)} %convert_element_type.14), channel_id=1, source_target_pairs={{3,0},{4,1},{5,2},{6,3},{7,4},{8,5},{9,6},{10,7},{11,8},{12,9},{13... | collective-permute-start | bytes 73736 | tf_op jit(solution)/shard_map/ppermute | solution.py:23
  137.8 4.6 %collective-permute-start.13 = (bf16[3,4096]{1,0:T(4,128)(2,1)S(1)}, bf16[3,4096]{1,0:T(4,128)(2,1)S(1)}, u32[]{:S(2)}, u32[]{:S(2)}) collective-permute-start(bf16[3,4096]{1,0:T(4,128)(2,1)S(1)} %convert_element_type.14), channel_id=1, source_target_pairs={{4,0},{5,1},{6,2},{7,3},{8,4},{9,5},{10,6},{11,7},{12,8},{13,9},{1... | collective-permute-start | bytes 73736 | tf_op jit(solution)/shard_map/ppermute | solution.py:23
  142.3 7.1 %collective-permute-start.14 = (bf16[3,4096]{1,0:T(4,128)(2,1)S(1)}, bf16[3,4096]{1,0:T(4,128)(2,1)S(1)}, u32[]{:S(2)}, u32[]{:S(2)}) collective-permute-start(bf16[3,4096]{1,0:T(4,128)(2,1)S(1)} %convert_element_type.14), channel_id=1, source_target_pairs={{5,0},{6,1},{7,2},{8,3},{9,4},{10,5},{11,6},{12,7},{13,8},{14,9},{... | collective-permute-start | bytes 73736 | tf_op jit(solution)/shard_map/ppermute | solution.py:23
  149.4 6.7 %collective-permute-start.1 = (f32[1,64,64]{1,2,0:T(8,128)S(1)}, f32[1,64,64]{1,2,0:T(8,128)S(1)}, u32[]{:S(2)}, u32[]{:S(2)}) collective-permute-start(f32[1,64,64]{1,2,0:T(8,128)S(1)} %convolution_bitcast_fusion.8), channel_id=1, source_target_pairs={{0,2},{1,3},{2,0},{3,1},{4,6},{5,7},{6,4},{7,5},{8,10},{9,11},{10,... | collective-permute-start | bytes 49160 | tf_op jit(solution)/shard_map/ppermute | solution.py:17
  164.5 9.8 %collective-permute-start.2 = (f32[1,64,64]{1,2,0:T(8,128)S(1)}, f32[1,64,64]{1,2,0:T(8,128)S(1)}, u32[]{:S(2)}, u32[]{:S(2)}) collective-permute-start(f32[1,64,64]{1,2,0:T(8,128)S(1)} %convolution_bitcast_fusion.6), channel_id=1, source_target_pairs={{0,4},{1,5},{2,6},{3,7},{4,0},{5,1},{6,2},{7,3},{8,12},{9,13},{10,... | collective-permute-start | bytes 49160 | tf_op jit(solution)/shard_map/ppermute | solution.py:17
  182.8 9.2 %collective-permute-start.3 = (f32[1,64,64]{1,2,0:T(8,128)S(1)}, f32[1,64,64]{1,2,0:T(8,128)S(1)}, u32[]{:S(2)}, u32[]{:S(2)}) collective-permute-start(f32[1,64,64]{1,2,0:T(8,128)S(1)} %convolution_bitcast_fusion.4), channel_id=1, source_target_pairs={{0,8},{1,9},{2,10},{3,11},{4,12},{5,13},{6,14},{7,15},{8,0},{9,1},... | collective-permute-start | bytes 49160 | tf_op jit(solution)/shard_map/ppermute | solution.py:17
  200.5 5.6 %collective-permute-start.4 = (f32[1,64,64]{1,2,0:T(8,128)S(1)}, f32[1,64,64]{1,2,0:T(8,128)S(1)}, u32[]{:S(2)}, u32[]{:S(2)}) collective-permute-start(f32[1,64,64]{1,2,0:T(8,128)S(1)} %convolution_bitcast_fusion.2), channel_id=1, source_target_pairs={{0,16},{1,17},{2,18},{3,19},{4,20},{5,21},{6,22},{7,23},{8,24},{9,... | collective-permute-start | bytes 49160 | tf_op jit(solution)/shard_map/ppermute | solution.py:17
  206.0 32.5 %collective-permute-start.21 = (bf16[3,64,1024]{2,1,0:T(8,128)(2,1)}, bf16[3,64,1024]{2,1,0:T(8,128)(2,1)S(1)}, u32[]{:S(2)}, u32[]{:S(2)}) collective-permute-start(bf16[3,64,1024]{2,1,0:T(8,128)(2,1)} %pad_maximum_fusion.1), channel_id=1, source_target_pairs={{0,1},{1,2},{2,3},{3,4},{4,5},{5,6},{6,7},{7,8},{8,9},{9,10},{10,1... | collective-permute-start | bytes 1179656 | tf_op jit(solution)/shard_map/ppermute | solution.py:23
  226.3 15.7 %collective-permute-start.22 = (bf16[3,64,1024]{2,1,0:T(8,128)(2,1)}, bf16[3,64,1024]{2,1,0:T(8,128)(2,1)S(1)}, u32[]{:S(2)}, u32[]{:S(2)}) collective-permute-start(bf16[3,64,1024]{2,1,0:T(8,128)(2,1)} %pad_maximum_fusion.1), channel_id=1, source_target_pairs={{1,0},{2,1},{3,2},{4,3},{5,4},{6,5},{7,6},{8,7},{9,8},{10,9},{11,1... | collective-permute-start | bytes 1179656 | tf_op jit(solution)/shard_map/ppermute | solution.py:23
  229.3 58.3 %collective-permute-start.23 = (bf16[3,64,1024]{2,1,0:T(8,128)(2,1)}, bf16[3,64,1024]{2,1,0:T(8,128)(2,1)S(1)}, u32[]{:S(2)}, u32[]{:S(2)}) collective-permute-start(bf16[3,64,1024]{2,1,0:T(8,128)(2,1)} %pad_maximum_fusion.1), channel_id=1, source_target_pairs={{2,0},{3,1},{4,2},{5,3},{6,4},{7,5},{8,6},{9,7},{10,8},{11,9},{12,... | collective-permute-start | bytes 1179656 | tf_op jit(solution)/shard_map/ppermute | solution.py:23
  232.4 57.5 %collective-permute-start.24 = (bf16[3,64,1024]{2,1,0:T(8,128)(2,1)}, bf16[3,64,1024]{2,1,0:T(8,128)(2,1)S(1)}, u32[]{:S(2)}, u32[]{:S(2)}) collective-permute-start(bf16[3,64,1024]{2,1,0:T(8,128)(2,1)} %pad_maximum_fusion.1), channel_id=1, source_target_pairs={{3,0},{4,1},{5,2},{6,3},{7,4},{8,5},{9,6},{10,7},{11,8},{12,9},{13... | collective-permute-start | bytes 1179656 | tf_op jit(solution)/shard_map/ppermute | solution.py:23
  235.4 55.2 %collective-permute-start.25 = (bf16[3,64,1024]{2,1,0:T(8,128)(2,1)}, bf16[3,64,1024]{2,1,0:T(8,128)(2,1)S(1)}, u32[]{:S(2)}, u32[]{:S(2)}) collective-permute-start(bf16[3,64,1024]{2,1,0:T(8,128)(2,1)} %pad_maximum_fusion.1), channel_id=1, source_target_pairs={{4,0},{5,1},{6,2},{7,3},{8,4},{9,5},{10,6},{11,7},{12,8},{13,9},{1... | collective-permute-start | bytes 1179656 | tf_op jit(solution)/shard_map/ppermute | solution.py:23
  238.5 52.9 %collective-permute-start.26 = (bf16[3,64,1024]{2,1,0:T(8,128)(2,1)}, bf16[3,64,1024]{2,1,0:T(8,128)(2,1)S(1)}, u32[]{:S(2)}, u32[]{:S(2)}) collective-permute-start(bf16[3,64,1024]{2,1,0:T(8,128)(2,1)} %pad_maximum_fusion.1), channel_id=1, source_target_pairs={{5,0},{6,1},{7,2},{8,3},{9,4},{10,5},{11,6},{12,7},{13,8},{14,9},{... | collective-permute-start | bytes 1179656 | tf_op jit(solution)/shard_map/ppermute | solution.py:23
  241.9 60.6 %collective-permute-start.15 = (bf16[512,1024]{1,0:T(8,128)(2,1)}, bf16[512,1024]{1,0:T(8,128)(2,1)}, u32[]{:S(2)}, u32[]{:S(2)}) collective-permute-start(bf16[512,1024]{1,0:T(8,128)(2,1)} %param.20), channel_id=1, source_target_pairs={{0,1},{1,2},{2,3},{3,4},{4,5},{5,6},{6,7},{7,8},{8,9},{9,10},{10,1... | collective-permute-start | bytes 3145736 | tf_op jit(solution)/shard_map/ppermute | solution.py:34
  287.6 24.8 %collective-permute-start.16 = (bf16[512,1024]{1,0:T(8,128)(2,1)}, bf16[512,1024]{1,0:T(8,128)(2,1)}, u32[]{:S(2)}, u32[]{:S(2)}) collective-permute-start(bf16[512,1024]{1,0:T(8,128)(2,1)} %param.20), channel_id=1, source_target_pairs={{1,0},{2,1},{3,2},{4,3},{5,4},{6,5},{7,6},{8,7},{9,8},{10,9},{11,1... | collective-permute-start | bytes 3145736 | tf_op jit(solution)/shard_map/ppermute | solution.py:36
where the time goes:
time: 403 us; the launch traced here: 397 us
  other arithmetic  110 us (27%)
  starting transfers between devices  86.1 us (21%)
  waiting for transfers between devices  68.5 us (17%)
  local copies, waits for them, and re-layouts  52.9 us (13%)
  loops' own time  39.2 us (10%)
  matrix products  38.9 us (10%)
    ppermute x20, starting transfers between devices, shifted(): return lax.ppermute(block, axis, route)  54.7 us
    ppermute x20, waiting for transfers between devices, shifted(): return lax.ppermute(block, axis, route)  51 us
    another operation x15, other arithmetic, lower_solve(): jax.scipy.linalg.solve_triangular(matrix, column, lower=True)  47.5 us
    another operation x1, loops' own time, body(): lax.fori_loop(0, near_slots, accumulate, jnp.zeros((leaf_count, leaf_poin...  39.2 us
    another operation x15, other arithmetic, body(): lower_now = jnp.linalg.cholesky(up_term + partner)  32.6 us
    dot_general x10, matrix products, accumulate(): jnp.dot(near_blocks[block_index], source_rows, preferred_element_type=jnp...  20.7 us
    unnamed x40, local copies, waits for them, and re-layouts  20.3 us
    ppermute x1, starting transfers between devices, padded(): lax.ppermute(tail, axis, [(i, (i + 1) % count) for i in range(ends)])  17.9 us
  transfers between devices with their start and end apart: 27, of which 12 were waited for; matrix products, arithmetic and copies ran while one was open for 28% of the time, Pallas kernels for 0%

commit v1 on v0

v1 whole, which is shorter than its diff:
```python
import jax
import jax.numpy as jnp
from jax import lax
from jax.experimental import pallas as pl
from jax.experimental.pallas import tpu as pltpu
from jax.sharding import PartitionSpec as P

AXES = ("row", "col")
HI = lax.Precision.HIGHEST
F32 = jnp.float32
BF16 = jnp.bfloat16
MESH = pl.DeviceIdType.MESH
PANEL = 8
SENDS = (
    (2, 1, 2, 2),
    (-2, 1, 2, 4),
    (3, 2, 2, 6),
    (-3, 0, 2, 8),
    (1, 1, 1, 0),
    (-1, 2, 1, 1),
    (5, 0, 1, 12),
    (-5, 0, 1, 13),
    (4, 0, 1, 10),
    (-4, 0, 1, 11),
)
SLOTS = 14


def mm(a, b, ca=1, cb=0, precision=HI):
    return lax.dot_general(
        a, b, (((ca,), (cb,)), ((), ())), precision=precision, preferred_element_type=F32
    )


def factor(grams):
    n = grams[0].shape[0]
    row = lax.broadcasted_iota(jnp.int32, (n, n), 0)
    col = lax.broadcasted_iota(jnp.int32, (n, n), 1)
    eye = jnp.where(row == col, 1.0, 0.0).astype(F32)
    wide = 2 * n
    top_row = lax.broadcasted_iota(jnp.int32, (PANEL, wide), 0)
    rest_row = lax.broadcasted_iota(jnp.int32, (n - PANEL, wide), 0) + PANEL
    start = tuple(jnp.concatenate([g, eye], axis=1) for g in grams)

    def panel(p, mats):
        live = rest_row < n - PANEL * p
        out = []
        for m in mats:
            top, rest = m[:PANEL], m[PANEL:]
            ctop = [jnp.broadcast_to(top[:, k : k + 1], (PANEL, wide)) for k in range(PANEL)]
            crest = [jnp.broadcast_to(rest[:, k : k + 1], (n - PANEL, wide)) for k in range(PANEL)]
            for j in range(PANEL):
                r = lax.rsqrt(ctop[j][j : j + 1])
                nj = top[j : j + 1] * r
                lt = ctop[j] * r
                lr = jnp.where(live, crest[j] * r, 0.0)
                top = jnp.where(
                    top_row > j, top - lt * nj, jnp.where(top_row == j, nj, top)
                )
                rest = rest - lr * nj
                for k in range(j + 1, PANEL):
                    lk = lt[k : k + 1]
                    ctop[k] = ctop[k] - lt * lk
                    crest[k] = crest[k] - lr * lk
            out.append(pltpu.roll(jnp.concatenate([rest, top], axis=0), wide - PANEL, 1))
        return tuple(out)

    done = lax.fori_loop(0, n // PANEL, panel, start)
    return [(jnp.where(col >= row, m[:, n:], 0.0), m[:, :n]) for m in done]


def tree_kernel(
    shape,
    levels,
    basis_ref,
    child_ref,
    upper_ref,
    vec_ref,
    ortho_ref,
    child_new_ref,
    top_new_ref,
    lower_ref,
    window_ref,
    table_ref,
    x_ref,
    stack_ref,
    term_ref,
    got_ref,
    x_sem,
    send_sem,
    recv_sem,
):
    rows, cols = shape
    total = rows * cols
    me = lax.axis_index("row") * cols + lax.axis_index("col")

    def place(distance):
        other = lax.rem(me + distance + total, total)
        return (other // cols, lax.rem(other, cols))

    def partner(level):
        step = 2**level
        other = me + step * (1 - 2 * lax.rem(me // step, 2))
        return (other // cols, lax.rem(other, cols))

    load = pltpu.make_async_copy(vec_ref, x_ref, x_sem)
    load.start()
    barrier = pltpu.get_barrier_semaphore()
    for send in SENDS:
        pl.semaphore_signal(barrier, inc=1, device_id=place(send[0]), device_id_type=MESH)
    for level in range(levels):
        pl.semaphore_signal(barrier, inc=1, device_id=partner(level), device_id_type=MESH)
    pl.semaphore_wait(barrier, len(SENDS) + levels)

    copies = []

    def send(src, dst, where):
        at = len(copies)
        copy = pltpu.make_async_remote_copy(
            src_ref=src,
            dst_ref=dst,
            send_sem=send_sem.at[at],
            recv_sem=recv_sem.at[at],
            device_id=where,
            device_id_type=MESH,
        )
        copy.start()
        copies.append(copy)
        return copy

    send(vec_ref, window_ref.at[0], place(1))
    send(vec_ref, window_ref.at[1], place(-1))

    leaf_count, rank, points = basis_ref.shape
    nvec = x_ref.shape[1]
    pad = jnp.zeros((rank, rank), BF16)

    def pack(entry, coeff, lower_t):
        stack_ref[entry, :, :nvec] = coeff.astype(BF16)
        stack_ref[entry, :, nvec:] = jnp.concatenate([lower_t.astype(BF16), pad], axis=1)

    leaves = factor([mm(basis_ref[l], basis_ref[l], 1, 1) for l in range(leaf_count)])
    ortho = [mm(leaves[l][1], basis_ref[l]) for l in range(leaf_count)]
    lifted = [mm(leaves[l][0], child_ref[l]) for l in range(leaf_count)]
    node_gram = mm(lifted[0], lifted[0], 0, 0) + mm(lifted[1], lifted[1], 0, 0)
    for l in range(leaf_count):
        ortho_ref[l] = ortho[l]
        lower_ref[l] = leaves[l][0]
    load.wait()
    coeffs = []
    for l in range(leaf_count):
        coeff = mm(
            ortho[l].astype(BF16), x_ref[l * points : (l + 1) * points, :], precision=None
        )
        coeffs.append(coeff)
        pack(1 + l, coeff, leaves[l][0])
    for distance, first, count, slot in SENDS:
        if first == 1 or (first == 2 and count == 1):
            send(
                stack_ref.at[pl.ds(first, count)], table_ref.at[pl.ds(slot, count)], place(distance)
            )
    ((lower_t, inverse),) = factor([node_gram])
    lower_ref[leaf_count] = lower_t
    fresh = [mm(lifted[l], inverse, 1, 1) for l in range(leaf_count)]
    for l in range(leaf_count):
        child_new_ref[l] = fresh[l]
    node_coeff = mm(fresh[0], coeffs[0], 0, 0) + mm(fresh[1], coeffs[1], 0, 0)
    pack(0, node_coeff, lower_t)
    pack(3, node_coeff, lower_t)
    for distance, first, count, slot in SENDS:
        if not (first == 1 or (first == 2 and count == 1)):
            send(
                stack_ref.at[pl.ds(first, count)], table_ref.at[pl.ds(slot, count)], place(distance)
            )
    for level in range(levels):
        up = mm(lower_t, upper_ref[level])
        term = mm(up, up, 0, 0)
        term_ref[level] = term
        copy = send(term_ref.at[level], got_ref.at[level], partner(level))
        copy.wait_recv()
        ((lower_t, inverse),) = factor([term + got_ref[level]])
        top_new_ref[level] = mm(up, inverse, 1, 1)
    for at, copy in enumerate(copies):
        copy.wait_send()
        if at < 2 + len(SENDS):
            copy.wait_recv()


def apply_kernel(
    shape,
    blocks_ref,
    window_ref,
    vec_ref,
    ortho_ref,
    child_ref,
    lower_ref,
    table_ref,
    coupling_ref,
    near_rows,
    near_cols,
    near_counts,
    far_rows,
    far_cols,
    far_counts,
    coupling_new_ref,
    product_ref,
    near_ref,
    far_ref,
    desc_ref,
):
    me = lax.axis_index("row") * shape[1] + lax.axis_index("col")
    slots, points, _ = blocks_ref.shape
    leaf_count, rank, _ = ortho_ref.shape
    nvec = vec_ref.shape[1]
    reach = window_ref.shape[1] // points
    near_ref[...] = jnp.zeros_like(near_ref)
    for b in range(slots):

        @pl.when(b < near_counts[0])
        def _():
            r = near_rows[b] - me * leaf_count
            c = near_cols[b] - me * leaf_count + reach
            near_ref[
                pl.ds(pl.multiple_of(r * points, points), points),
                pl.ds(pl.multiple_of(c * points, points), points),
            ] = blocks_ref[b]

    far_ref[...] = jnp.zeros_like(far_ref)
    split = coupling_ref.shape[0] * leaf_count // (leaf_count + 1)
    for b in range(coupling_ref.shape[0]):
        upper = b >= split
        if upper:
            active = b - split < far_counts[0, 1]
            row = leaf_count
            delta = far_cols[b] - me
            slot = jnp.where(
                delta == -3,
                7,
                jnp.where(
                    delta == 3,
                    8,
                    jnp.where(
                        delta == -4, 10, jnp.where(delta == 4, 11, jnp.where(delta == -5, 12, 13))
                    ),
                ),
            )
        else:
            active = b < far_counts[0, 0]
            row = jnp.where(active, far_rows[b] - me * leaf_count, 0)
            delta = far_cols[b] - me * leaf_count
            odd = lax.rem(far_cols[b], 2)
            slot = jnp.where(
                delta < -4,
                6,
                jnp.where(
                    delta < -2,
                    2 + odd,
                    jnp.where(
                        delta < 0, 0, jnp.where(delta < 4, 1, jnp.where(delta < 6, 4 + odd, 9))
                    ),
                ),
            )
        slot = jnp.where(active, slot, 0)
        item = table_ref[slot]
        half = mm(lower_ref[row], coupling_ref[b])
        new = mm(half, item[:, nvec : nvec + rank].astype(F32), 1, 1)
        new = jnp.where(active, new, 0.0)
        coupling_new_ref[b] = new
        low = new.astype(BF16)
        term = mm(low, item[:, :nvec], precision=None)
        far_ref[row] = far_ref[row] + term
    for l in range(leaf_count):
        desc_ref[l] = (far_ref[l] + mm(child_ref[l], far_ref[leaf_count])).astype(BF16)
    tile = 256

    @pl.loop(0, nvec // tile)
    def _(step):
        at = pl.ds(pl.multiple_of(step * tile, tile), tile)
        side = reach * points
        acc = mm(near_ref[:, :side], window_ref[0, :, at], precision=None)
        acc = acc + mm(
            near_ref[:, side : side + leaf_count * points], vec_ref[:, at], precision=None
        )
        acc = acc + mm(
            near_ref[:, side + leaf_count * points :], window_ref[1, :, at], precision=None
        )
        for l in range(leaf_count):
            far = mm(ortho_ref[l].astype(BF16), desc_ref[l, :, at], 0, 0, precision=None)
            product_ref[l * points : (l + 1) * points, at] = (
                acc[l * points : (l + 1) * points] + far
            ).astype(BF16)


def body(
    shape,
    leaf_basis,
    child_transfer,
    top_transfer,
    vectors,
    near_blocks,
    near_rows,
    near_cols,
    near_counts,
    coupling,
    coupling_rows,
    coupling_cols,
    block_counts,
):
    leaf_count, rank, points = leaf_basis.shape
    nvec = vectors.shape[1]
    levels = top_transfer.shape[1]
    square = (rank, rank)
    vmem = pl.BlockSpec(memory_space=pltpu.VMEM)
    smem = pl.BlockSpec(memory_space=pltpu.SMEM)
    hbm = pl.BlockSpec(memory_space=pl.ANY)
    copies = 2 + len(SENDS) + levels
    held = nvec + 2 * rank

    def tree(*refs):
        tree_kernel(shape, levels, *refs)

    ortho, child_new, top_new, lowers, window, table = pl.pallas_call(
        tree,
        name="tree",
        out_shape=(
            jax.ShapeDtypeStruct(leaf_basis.shape, F32),
            jax.ShapeDtypeStruct((leaf_count,) + square, F32),
            jax.ShapeDtypeStruct((levels,) + square, F32),
            jax.ShapeDtypeStruct((leaf_count + 1,) + square, F32),
            jax.ShapeDtypeStruct((2,) + vectors.shape, BF16),
            jax.ShapeDtypeStruct((SLOTS, rank, held), BF16),
        ),
        in_specs=[vmem, vmem, vmem, hbm],
        out_specs=(vmem, vmem, vmem, vmem, hbm, hbm),
        scratch_shapes=[
            pltpu.VMEM(vectors.shape, BF16),
            pltpu.VMEM((4, rank, held), BF16),
            pltpu.VMEM((levels,) + square, F32),
            pltpu.VMEM((levels,) + square, F32),
            pltpu.SemaphoreType.DMA,
            pltpu.SemaphoreType.DMA((copies,)),
            pltpu.SemaphoreType.DMA((copies,)),
        ],
        compiler_params=pltpu.CompilerParams(
            collective_id=0, has_side_effects=True, vmem_limit_bytes=32 * 1024 * 1024
        ),
    )(
        leaf_basis,
        child_transfer.reshape((leaf_count,) + square),
        top_transfer.reshape((levels,) + square),
        vectors,
    )

    def apply(*refs):
        apply_kernel(shape, *refs)

    coupling_new, product = pl.pallas_call(
        apply,
        name="apply",
        out_shape=(
            jax.ShapeDtypeStruct((coupling.shape[0],) + square, F32),
            jax.ShapeDtypeStruct(vectors.shape, BF16),
        ),
        in_specs=[vmem] * 8 + [smem] * 6,
        out_specs=(vmem, vmem),
        scratch_shapes=[
            pltpu.VMEM((leaf_count * points, 3 * leaf_count * points), BF16),
            pltpu.VMEM((leaf_count + 1, rank, nvec), F32),
            pltpu.VMEM((leaf_count, rank, nvec), BF16),
        ],
        compiler_params=pltpu.CompilerParams(vmem_limit_bytes=48 * 1024 * 1024),
    )(
        near_blocks,
        window,
        vectors,
        ortho,
        child_new,
        lowers,
        table,
        coupling.reshape((-1,) + square),
        near_rows,
        near_cols,
        near_counts,
        coupling_rows,
        coupling_cols,
        block_counts,
    )
    return (
        ortho,
        child_new.reshape(leaf_count, -1),
        top_new.reshape(1, levels, -1),
        coupling_new.reshape(coupling.shape),
        product,
    )


def solution(mesh):
    shape = (mesh.shape["row"], mesh.shape["col"])
    ranks = (3, 2, 3, 2, 3, 1, 1, 1, 2, 1, 1, 2)

    def run(*args):
        return body(shape, *args)

    def spec(rank):
        return P(AXES, *([None] * (rank - 1)))

    return jax.shard_map(
        run,
        mesh=mesh,
        in_specs=tuple(spec(rank) for rank in ranks),
        out_specs=tuple(spec(rank) for rank in (3, 2, 3, 2, 2)),
        check_vma=False,
    )
```

time: 403 us -> 151 us (0.37); the launches traced: 397 us -> 150 us
  Pallas kernels: 0 us -> 132 us
  other arithmetic: 110 us -> 1.08 us
  starting transfers between devices: 86.1 us -> 0 us
  waiting for transfers between devices: 68.5 us -> 0 us
  loops' own time: 39.2 us -> 0 us
  matrix products: 38.9 us -> 0 us
  local copies, waits for them, and re-layouts: 52.9 us -> 16 us
    pallas_call x0 -> x2, Pallas kernels: none -> 132 us  [the longest x1 122 us: body(): pl.pallas_call(tree, name='tree', out_shape=(jax.ShapeDtypeStruct(leaf_ba...]
    another operation x38 -> x0, other arithmetic: 99.2 us -> none  [the longest x15 47.5 us: lower_solve(): jax.scipy.linalg.solve_triangular(matrix, column, lower=True)]
    ppermute x27 -> x0, starting transfers between devices: 86.1 us -> none  [the longest x20 54.7 us: shifted(): return lax.ppermute(block, axis, route)]
    ppermute x27 -> x0, waiting for transfers between devices: 68.5 us -> none  [the longest x20 51 us: shifted(): return lax.ppermute(block, axis, route)]
    another operation x1 -> x0, loops' own time: 39.2 us -> none  [body(): lax.fori_loop(0, near_slots, accumulate, jnp.zeros((leaf_count, leaf_poin...]
    dot_general x31 -> x0, matrix products: 37.1 us -> none  [the longest x10 20.7 us: accumulate(): jnp.dot(near_blocks[block_index], source_rows, preferred_element_type=jnp...]
    dynamic_slice x40 -> x0, local copies, waits for them, and re-layouts: 18.7 us -> none  [the longest x10 5.91 us: accumulate(): block_product = jnp.where(near_active[block_index], block_product, 0.0)]
    unnamed x40 -> x29, local copies, waits for them, and re-layouts: 20.3 us -> 8.87 us
  transfers between devices with their start and end apart: 27 -> 0, of which waited for: 12 -> 0; matrix products, arithmetic and copies ran while one was open for 28% -> 0% of each run, Pallas kernels for 0% -> 0%
where the time goes in v1:
time: 151 us; the launch traced here: 150 us
  Pallas kernels  132 us (87%)
  local copies, waits for them, and re-layouts  16 us (11%)
    pallas_call x1, Pallas kernels, body(): pl.pallas_call(tree, name='tree', out_shape=(jax.ShapeDtypeStruct(leaf_ba...  122 us
    pallas_call x1, Pallas kernels, body(): pl.pallas_call(apply, name='apply', out_shape=(jax.ShapeDtypeStruct((coup...  10 us
    unnamed x29, local copies, waits for them, and re-layouts  8.87 us

profile of v1, /device:TPU:0, one launch (start us, length us, event | category | flops | bytes accessed | tf_op | source)
XLA Modules:
  0.0 150.1 jit_solution(14141568507321288697)
XLA Ops:
  0.6 0.0 copy-start
  0.6 0.0 copy-start.12
  0.7 0.0 copy-start.11
  0.7 0.0 copy-start.10
  0.7 0.0 copy-start.9
  1.4 0.9 reshape.28.refs_1_
  2.3 1.1 reduce
  3.4 0.1 reshape.29.refs_2_
  3.5 1.9 %reshape.32.refs_7_ = f32[15,64,64]{2,1,0:T(8,128)} reshape(f32[15,4096]{1,0:T(8,128)} %param.20) | data formatting | bytes 491520 | tf_op jit(solution)/shard_map/reshape | solution.py:380
  5.4 0.0 copy-done
  5.4 0.0 copy-start.6
  5.4 0.9 copy-done.6
  6.3 121.5 %tree.1 = (f32[2,64,256]{2,1,0:T(8,128)S(1)}, f32[2,64,64]{2,1,0:T(8,128)S(1)}, f32[5,64,64]{2,1,0:T(8,128)S(1)}, f32[3,64,64]{2,1,0:T(8,128)S(1)}, bf16[2,512,1...) custom-call(f32[2,64,256]{2,1,0:T(8,128)S(1)} %copy-done.6, f32[2,64,64]{2,1,0:T(8,128)S(1)} %reshape.28.refs_1_, ...), custom_call_target="tpu_custom_call" | custom-call | tf_op jit(solution)/shard_map/tree/pallas_call | solution.py:322
  127.8 0.0 copy-start.1
  127.8 1.3 copy-done.1
  129.1 0.0 copy-start.5
  129.1 0.7 copy-done.5
  129.8 0.0 copy-start.7
  129.8 0.6 copy-done.7
  130.5 1.7 %reshape.34 = f32[1,5,4096]{2,0,1:T(1,128)} reshape(f32[5,64,64]{2,1,0:T(8,128)} %copy-done.5) | data formatting | bytes 163840 | tf_op jit(solution)/shard_map/reshape | solution.py:391
  132.1 0.7 reshape.30
  132.9 0.0 copy-done.12
  132.9 0.0 copy-done.11
  132.9 0.0 copy-done.10
  132.9 0.0 copy-done.9
  132.9 0.0 copy-start.2
  132.9 1.0 copy-done.2
  133.9 0.0 copy-start.3
  133.9 1.3 copy-done.3
  135.2 0.0 copy-start.8
  135.2 0.9 copy-done.8
  136.1 0.0 copy-start.13
  136.1 0.7 copy-done.13
  136.8 10.0 %apply.1 = (f32[15,64,64]{2,1,0:T(8,128)S(1)}, bf16[512,1024]{1,0:T(8,128)(2,1)}) custom-call(bf16[10,256,256]{2,1,0:T(8,128)(2,1)S(1)} %copy-done.3, bf16[2,512,1024]{2,1,0:T(8,128)(2,1)} %copy-done.1, bf16[512,1024]{1,0:T(8,128)(2,1)S(1)} %copy-done, f32[2,64,256]{2,1,0:T(8,128)S(1)} %get-tuple-element.36.refs_3_, ...), custom_call_target="tpu_custom_call" | custom-call | tf_op jit(solution)/shard_map/apply/pallas_call | solution.py:357
  146.8 0.0 copy-start.4
  146.8 0.8 copy-done.4
  147.6 1.9 %reshape.33 = f32[15,4096]{1,0:T(8,128)} reshape(f32[15,64,64]{2,1,0:T(8,128)} %copy-done.4) | data formatting | bytes 491520 | tf_op jit(solution)/shard_map/reshape | solution.py:392
  149.5 0.7 copy.21
Async XLA Ops:
  0.6 4.7 %copy-start = (bf16[512,1024]{1,0:T(8,128)(2,1)S(1)}, bf16[512,1024]{1,0:T(8,128)(2,1)}, u32[]{:S(2)}) copy-start(bf16[512,1024]{1,0:T(8,128)(2,1)} %refs_2_.1) | copy-start | bytes 3145732
  0.6 132.2 %copy-start.12 = (s32[15]{0:T(128)S(1)}, s32[15]{0:T(128)}, u32[]{:S(2)}) copy-start(s32[15]{0:T(128)} %refs_12_.1) | copy-start | bytes 184
  0.7 132.2 %copy-start.11 = (s32[15]{0:T(128)S(1)}, s32[15]{0:T(128)}, u32[]{:S(2)}) copy-start(s32[15]{0:T(128)} %refs_11_.1) | copy-start | bytes 184
  0.7 132.2 %copy-start.10 = (s32[10]{0:T(128)S(1)}, s32[10]{0:T(128)}, u32[]{:S(2)}) copy-start(s32[10]{0:T(128)} %refs_9_.1) | copy-start | bytes 124
  0.7 132.2 %copy-start.9 = (s32[10]{0:T(128)S(1)}, s32[10]{0:T(128)}, u32[]{:S(2)}) copy-start(s32[10]{0:T(128)} %refs_8_.1) | copy-start | bytes 124
  5.4 0.9 copy-start.6
  127.8 1.3 copy-start.1
  129.1 0.7 copy-start.5
  129.8 0.6 copy-start.7
  132.9 1.0 copy-start.2
  133.9 1.3 copy-start.3
  135.2 0.9 copy-start.8
  136.1 0.7 copy-start.13
  146.8 0.8 copy-start.4

commit v2 on v1

--- a/solution.py
+++ b/solution.py
@@ -24,6 +24,10 @@
     (-4, 0, 1, 11),
 )
 SLOTS = 14
+RELAY_COLS = 4
+RELAY_SLOTS = 38
+NEEDED = {1: (0, 1), 2: (0, 2), 3: (1, 2), 4: (2, 1), 5: (2, 1)}
+NEEDED_BACK = {1: (1, 1), 2: (0, 2), 3: (0, 3), 4: (2, 1), 5: (2, 1)}
 
 
 def mm(a, b, ca=1, cb=0, precision=HI):
@@ -103,20 +107,28 @@
         other = me + step * (1 - 2 * lax.rem(me // step, 2))
         return (other // cols, lax.rem(other, cols))
 
+    relay = cols == RELAY_COLS
+    here, z = me // cols, lax.rem(me, cols)
+
+    def beside(rows_off, cols_off):
+        return (lax.rem(here + rows_off + rows, rows), lax.rem(z + cols_off + cols, cols))
+
     load = pltpu.make_async_copy(vec_ref, x_ref, x_sem)
     load.start()
     barrier = pltpu.get_barrier_semaphore()
-    for send in SENDS:
-        pl.semaphore_signal(barrier, inc=1, device_id=place(send[0]), device_id_type=MESH)
-    for level in range(levels):
-        pl.semaphore_signal(barrier, inc=1, device_id=partner(level), device_id_type=MESH)
-    pl.semaphore_wait(barrier, len(SENDS) + levels)
-
-    copies = []
-
-    def send(src, dst, where):
-        at = len(copies)
-        copy = pltpu.make_async_remote_copy(
+    if relay:
+        peers = [place(1), place(-1)]
+        peers += [beside(0, 1), beside(0, -1)]
+        peers += [beside(1, 0), beside(-1, 0), beside(2, 0), beside(-2, 0)]
+    else:
+        peers = [place(send[0]) for send in SENDS]
+    peers += [partner(level) for level in range(levels)]
+    for peer in peers:
+        pl.semaphore_signal(barrier, inc=1, device_id=peer, device_id_type=MESH)
+    pl.semaphore_wait(barrier, len(peers))
+
+    def remote(at, src, dst, where):
+        return pltpu.make_async_remote_copy(
             src_ref=src,
             dst_ref=dst,
             send_sem=send_sem.at[at],
@@ -124,15 +136,113 @@
             device_id=where,
             device_id_type=MESH,
         )
-        copy.start()
-        copies.append(copy)
-        return copy
-
-    send(vec_ref, window_ref.at[0], place(1))
-    send(vec_ref, window_ref.at[1], place(-1))
 
     leaf_count, rank, points = basis_ref.shape
     nvec = x_ref.shape[1]
+    half = vec_ref.shape[0] // 2
+
+    def vector_copy(part, side):
+        at = pl.ds(part * half, half)
+        return remote(
+            2 * part + side, vec_ref.at[at], window_ref.at[side, at], place(1 - 2 * side)
+        )
+
+    vector_copies = [vector_copy(part, side) for part in range(2) for side in range(2)]
+    vector_copies[0].start()
+    vector_copies[1].start()
+
+    def direct_copy(index):
+        distance, first, count, slot = SENDS[index]
+        return remote(
+            4 + index,
+            stack_ref.at[pl.ds(first, count)],
+            table_ref.at[pl.ds(slot, count)],
+            place(distance),
+        )
+
+    def own_row(source, first=0, count=3):
+        return table_ref.at[pl.ds((cols + source) * 3 + first, count)]
+
+    def hop(stage, side):
+        way = 1 - 2 * side
+        at = own_row(z - way * stage)
+        return remote(4 + 2 * stage + side, at, at, beside(0, way))
+
+    def hop_in(stage, side):
+        way = 1 - 2 * side
+        at = own_row(z - way * (stage + 1))
+        return remote(4 + 2 * stage + side, at, at, beside(0, way))
+
+    def sends_hop(stage, side):
+        if side == 0:
+            return jnp.logical_and(z >= stage, z < cols - 1)
+        return jnp.logical_and(z < cols - stage, z > 0)
+
+    def gets_hop(stage, side):
+        return z > stage if side == 0 else z < cols - 1 - stage
+
+    def row_copies(column, source):
+        found = []
+        ahead, back = cols + column - source, cols - column + source
+        if ahead in NEEDED:
+            first, count = NEEDED[ahead]
+            found.append(
+                remote(
+                    10 + source,
+                    own_row(source, first, count),
+                    table_ref.at[pl.ds(source * 3 + first, count)],
+                    beside(1, 0),
+                )
+            )
+        if back in NEEDED_BACK:
+            first, count = NEEDED_BACK[back]
+            found.append(
+                remote(
+                    14 + source,
+                    own_row(source, first, count),
+                    table_ref.at[pl.ds((2 * cols + source) * 3 + first, count)],
+                    beside(-1, 0),
+                )
+            )
+        if column == 0 and source == cols - 1:
+            found.append(
+                remote(
+                    18, own_row(source, 2, 1), table_ref.at[pl.ds(9 * cols, 1)], beside(2, 0)
+                )
+            )
+        if column == cols - 1 and source == 0:
+            found.append(
+                remote(
+                    19, own_row(source, 2, 1), table_ref.at[pl.ds(9 * cols + 1, 1)], beside(-2, 0)
+                )
+            )
+        return found
+
+    def start_rows(away):
+        for column in range(cols):
+            sources = sorted({column - away, column + away})
+
+            @pl.when(z == column)
+            def _():
+                for source in sources:
+                    if 0 <= source < cols:
+                        for copy in row_copies(column, source):
+                            copy.start()
+
+    def start_hops(stage):
+        for side in range(2):
+
+            @pl.when(sends_hop(stage, side))
+            def _():
+                hop(stage, side).start()
+
+    def take_hops(stage):
+        for side in range(2):
+
+            @pl.when(gets_hop(stage, side))
+            def _():
+                hop_in(stage, side).wait_recv()
+
     pad = jnp.zeros((rank, rank), BF16)
 
     def pack(entry, coeff, lower_t):
@@ -154,11 +264,6 @@
         )
         coeffs.append(coeff)
         pack(1 + l, coeff, leaves[l][0])
-    for distance, first, count, slot in SENDS:
-        if first == 1 or (first == 2 and count == 1):
-            send(
-                stack_ref.at[pl.ds(first, count)], table_ref.at[pl.ds(slot, count)], place(distance)
-            )
     ((lower_t, inverse),) = factor([node_gram])
     lower_ref[leaf_count] = lower_t
     fresh = [mm(lifted[l], inverse, 1, 1) for l in range(leaf_count)]
@@ -167,23 +272,64 @@
     node_coeff = mm(fresh[0], coeffs[0], 0, 0) + mm(fresh[1], coeffs[1], 0, 0)
     pack(0, node_coeff, lower_t)
     pack(3, node_coeff, lower_t)
-    for distance, first, count, slot in SENDS:
-        if not (first == 1 or (first == 2 and count == 1)):
-            send(
-                stack_ref.at[pl.ds(first, count)], table_ref.at[pl.ds(slot, count)], place(distance)
-            )
+    if relay:
+        keep = pltpu.make_async_copy(stack_ref.at[pl.ds(1, 3)], own_row(z), x_sem)
+        keep.start()
+        keep.wait()
+        start_hops(0)
+        start_rows(0)
+    else:
+        for index in range(len(SENDS)):
+            direct_copy(index).start()
+    vector_copies[2].start()
+    vector_copies[3].start()
+    exchanges = []
     for level in range(levels):
         up = mm(lower_t, upper_ref[level])
         term = mm(up, up, 0, 0)
         term_ref[level] = term
-        copy = send(term_ref.at[level], got_ref.at[level], partner(level))
+        copy = remote(20 + level, term_ref.at[level], got_ref.at[level], partner(level))
+        copy.start()
+        exchanges.append(copy)
+        if relay and level in (2, 4):
+            take_hops(level // 2 - 1)
+            start_hops(level // 2)
+            start_rows(level // 2)
         copy.wait_recv()
         ((lower_t, inverse),) = factor([term + got_ref[level]])
         top_new_ref[level] = mm(up, inverse, 1, 1)
-    for at, copy in enumerate(copies):
+    if relay:
+        for stage in range(cols - 1):
+            if 2 * stage + 2 >= levels:
+                take_hops(stage)
+                if stage + 1 < cols - 1:
+                    start_hops(stage + 1)
+                start_rows(stage + 1)
+        for stage in range(cols - 1):
+            for side in range(2):
+
+                @pl.when(sends_hop(stage, side))
+                def _():
+                    hop(stage, side).wait_send()
+
+        for column in range(cols):
+
+            @pl.when(z == column)
+            def _():
+                for source in range(cols):
+                    for copy in row_copies(column, source):
+                        copy.wait_send()
+                for source in range(cols):
+                    for copy in row_copies(column, source):
+                        copy.wait_recv()
+
+    else:
+        for index in range(len(SENDS)):
+            direct_copy(index).wait()
+    for copy in exchanges:
         copy.wait_send()
-        if at < 2 + len(SENDS):
-            copy.wait_recv()
+    for copy in vector_copies:
+        copy.wait()
 
 
 def apply_kernel(
@@ -260,7 +406,16 @@
                     ),
                 ),
             )
-        slot = jnp.where(active, slot, 0)
+        if shape[1] == RELAY_COLS:
+            cols = shape[1]
+            span = 1 if upper else leaf_count
+            entry = leaf_count if upper else lax.rem(far_cols[b], leaf_count)
+            source = jnp.where(active, far_cols[b] // span, me)
+            apart = source // cols - me // cols
+            slot = ((apart + 1) * cols + lax.rem(source, cols)) * 3 + entry
+            slot = jnp.where(apart < -1, 9 * cols, jnp.where(apart > 1, 9 * cols + 1, slot))
+        else:
+            slot = jnp.where(active, slot, 0)
         item = table_ref[slot]
         half = mm(lower_ref[row], coupling_ref[b])
         new = mm(half, item[:, nvec : nvec + rank].astype(F32), 1, 1)
@@ -313,7 +468,8 @@
     vmem = pl.BlockSpec(memory_space=pltpu.VMEM)
     smem = pl.BlockSpec(memory_space=pltpu.SMEM)
     hbm = pl.BlockSpec(memory_space=pl.ANY)
-    copies = 2 + len(SENDS) + levels
+    copies = 20 + levels
+    slots = RELAY_SLOTS if shape[1] == RELAY_COLS else SLOTS
     held = nvec + 2 * rank
 
     def tree(*refs):
@@ -328,7 +484,7 @@
             jax.ShapeDtypeStruct((levels,) + square, F32),
             jax.ShapeDtypeStruct((leaf_count + 1,) + square, F32),
             jax.ShapeDtypeStruct((2,) + vectors.shape, BF16),
-            jax.ShapeDtypeStruct((SLOTS, rank, held), BF16),
+            jax.ShapeDtypeStruct((slots, rank, held), BF16),
         ),
         in_specs=[vmem, vmem, vmem, hbm],
         out_specs=(vmem, vmem, vmem, vmem, hbm, hbm),

time: 151 us -> 129 us (0.85)
  Pallas kernels: 132 us -> 107 us
  local copies, waits for them, and re-layouts: 16 us -> 19.2 us
    pallas_call x1, Pallas kernels: 122 us -> 96.1 us  [body(): pl.pallas_call(tree, name='tree', out_shape=(jax.ShapeDtypeStruct(leaf_ba...]
    unnamed x29 -> x33, local copies, waits for them, and re-layouts: 8.87 us -> 11.4 us
where the time goes in v2:
time: 129 us
  Pallas kernels  107 us (83%)
  local copies, waits for them, and re-layouts  19.2 us (15%)
  between operations  1.47 us (1%)
    pallas_call x1, Pallas kernels, body(): pl.pallas_call(tree, name='tree', out_shape=(jax.ShapeDtypeStruct(leaf_ba...  96.1 us
    unnamed x33, local copies, waits for them, and re-layouts  11.4 us
    pallas_call x1, Pallas kernels, body(): pl.pallas_call(apply, name='apply', out_shape=(jax.ShapeDtypeStruct((coup...  11 us

profile of v2, /device:TPU:0, one launch (start us, length us, event | category | flops | bytes accessed | tf_op | source)
XLA Modules:
  0.0 128.9 jit_solution(9625696584848309187)
XLA Ops:
  0.6 0.0 copy-start.2
  0.6 0.0 copy-start.15
  0.7 0.0 copy-start.14
  0.7 0.0 copy-start.13
  0.7 0.0 copy-start.12
  0.7 0.0 copy-start.11
  1.4 1.5 %reshape.28.refs_1_ = f32[2,64,64]{2,1,0:T(8,128)} reshape(f32[2,4096]{1,0:T(2,128)} %param.13) | data formatting | bytes 65536 | tf_op jit(solution)/shard_map/reshape | solution.py:505
  2.9 1.1 reduce
  4.0 0.1 reshape.29.refs_2_
  4.1 1.9 %reshape.32.refs_7_ = f32[15,64,64]{2,1,0:T(8,128)} reshape(f32[15,4096]{1,0:T(8,128)} %param.20) | data formatting | bytes 491520 | tf_op jit(solution)/shard_map/reshape | solution.py:536
  6.0 0.0 copy-start.1
  6.0 1.2 copy-done.1
  7.2 0.0 copy-start.6
  7.2 0.8 copy-done.6
  8.1 0.0 copy-start.8
  8.1 0.9 copy-done.8
  9.0 96.1 %tree.1 = (f32[2,64,256]{2,1,0:T(8,128)S(1)}, f32[2,64,64]{2,1,0:T(8,128)S(1)}, f32[5,64,64]{2,1,0:T(8,128)S(1)}, f32[3,64,64]{2,1,0:T(8,128)S(1)}, bf16[2,512,1...) custom-call(f32[2,64,256]{2,1,0:T(8,128)S(1)} %copy-done.8, f32[2,64,64]{2,1,0:T(8,128)S(1)} %copy-done.6, ...), custom_call_target="tpu_custom_call" | custom-call | tf_op jit(solution)/shard_map/tree/pallas_call | solution.py:478
  105.1 0.0 copy-start
  105.1 2.4 %copy-done = bf16[38,64,1152]{2,1,0:T(8,128)(2,1)} copy-done((bf16[38,64,1152]{2,1,0:T(8,128)(2,1)}, bf16[38,64,1152]{2,1,0:T(8,128)(2,1)S(1)}, u32[]{:S(2)}) %copy-start) | copy-done | bytes 5603352
  107.6 0.0 copy-start.7
  107.6 0.7 copy-done.7
  108.2 0.0 copy-start.9
  108.2 0.6 copy-done.9
  108.9 1.7 %reshape.34 = f32[1,5,4096]{2,0,1:T(1,128)} reshape(f32[5,64,64]{2,1,0:T(8,128)} %copy-done.7) | data formatting | bytes 163840 | tf_op jit(solution)/shard_map/reshape | solution.py:547
  110.6 0.7 reshape.30
  111.3 0.0 copy-done.2
  111.3 0.0 copy-done.15
  111.3 0.0 copy-done.14
  111.3 0.0 copy-done.13
  111.3 0.0 copy-done.12
  111.3 0.0 copy-done.11
  111.3 0.0 copy-start.3
  111.3 1.0 copy-done.3
  112.3 0.0 copy-start.4
  112.3 1.3 %copy-done.4 = bf16[10,256,256]{2,1,0:T(8,128)(2,1)S(1)} copy-done((bf16[10,256,256]{2,1,0:T(8,128)(2,1)S(1)}, bf16[10,256,256]{2,1,0:T(8,128)(2,1)}, u32[]{:S(2)}) %copy-start.4) | copy-done | bytes 1310744
  113.7 0.0 copy-start.10
  113.7 0.9 copy-done.10
  114.6 11.0 %apply.1 = (f32[15,64,64]{2,1,0:T(8,128)S(1)}, bf16[512,1024]{1,0:T(8,128)(2,1)}) custom-call(bf16[10,256,256]{2,1,0:T(8,128)(2,1)S(1)} %copy-done.4, bf16[2,512,1024]{2,1,0:T(8,128)(2,1)S(1)} %get-tuple-element.16.refs_1_, bf16[512,1024]{1,0:T(8,128)(2,1)S(1)} %copy-done.2, f32[2,64,256]{2,1,0:T(8,128)S(1)} %get-tuple-element.36.refs_3_, ...), custom_call_target="tpu_custom_call" | custom-call | tf_op jit(solution)/shard_map/apply/pallas_call | solution.py:513
  125.6 0.0 copy-start.5
  125.6 0.8 copy-done.5
  126.3 1.9 %reshape.33 = f32[15,4096]{1,0:T(8,128)} reshape(f32[15,64,64]{2,1,0:T(8,128)} %copy-done.5) | data formatting | bytes 491520 | tf_op jit(solution)/shard_map/reshape | solution.py:548
  128.2 0.7 copy.21
Async XLA Ops:
  0.6 110.6 %copy-start.2 = (bf16[512,1024]{1,0:T(8,128)(2,1)S(1)}, bf16[512,1024]{1,0:T(8,128)(2,1)}, u32[]{:S(2)}) copy-start(bf16[512,1024]{1,0:T(8,128)(2,1)} %refs_2_.1) | copy-start | bytes 3145732
  0.6 110.6 %copy-start.15 = (s32[1,2]{1,0:T(1,128)S(1)}, s32[1,2]{1,0:T(1,128)}, u32[]{:S(2)}) copy-start(s32[1,2]{1,0:T(1,128)} %refs_13_.1) | copy-start | bytes 28
  0.7 110.6 %copy-start.14 = (s32[15]{0:T(128)S(1)}, s32[15]{0:T(128)}, u32[]{:S(2)}) copy-start(s32[15]{0:T(128)} %refs_12_.1) | copy-start | bytes 184
  0.7 110.6 %copy-start.13 = (s32[15]{0:T(128)S(1)}, s32[15]{0:T(128)}, u32[]{:S(2)}) copy-start(s32[15]{0:T(128)} %refs_11_.1) | copy-start | bytes 184
  0.7 110.6 %copy-start.12 = (s32[10]{0:T(128)S(1)}, s32[10]{0:T(128)}, u32[]{:S(2)}) copy-start(s32[10]{0:T(128)} %refs_9_.1) | copy-start | bytes 124
  0.7 110.6 %copy-start.11 = (s32[10]{0:T(128)S(1)}, s32[10]{0:T(128)}, u32[]{:S(2)}) copy-start(s32[10]{0:T(128)} %refs_8_.1) | copy-start | bytes 124
  6.0 1.2 copy-start.1
  7.2 0.8 copy-start.6
  8.1 0.9 copy-start.8
  105.1 2.4 %copy-start = (bf16[38,64,1152]{2,1,0:T(8,128)(2,1)}, bf16[38,64,1152]{2,1,0:T(8,128)(2,1)S(1)}, u32[]{:S(2)}) copy-start(bf16[38,64,1152]{2,1,0:T(8,128)(2,1)S(1)} %get-tuple-element.18.refs_6_) | copy-start | bytes 16809988
  107.6 0.7 copy-start.7
  108.2 0.6 copy-start.9
  111.3 1.0 copy-start.3
  112.3 1.3 %copy-start.4 = (bf16[10,256,256]{2,1,0:T(8,128)(2,1)S(1)}, bf16[10,256,256]{2,1,0:T(8,128)(2,1)}, u32[]{:S(2)}) copy-start(bf16[10,256,256]{2,1,0:T(8,128)(2,1)} %refs_0_.3) | copy-start | bytes 3932164
  113.7 0.9 copy-start.10
  125.6 0.8 copy-start.5

commit v3 on v2

--- a/solution.py
+++ b/solution.py
@@ -26,6 +26,8 @@
 SLOTS = 14
 RELAY_COLS = 4
 RELAY_SLOTS = 38
+RELAY_LEVELS = (0, 1)
+LATE_LEVEL = 2
 NEEDED = {1: (0, 1), 2: (0, 2), 3: (1, 2), 4: (2, 1), 5: (2, 1)}
 NEEDED_BACK = {1: (1, 1), 2: (0, 2), 3: (0, 3), 4: (2, 1), 5: (2, 1)}
 
@@ -34,6 +36,18 @@
     return lax.dot_general(
         a, b, (((ca,), (cb,)), ((), ())), precision=precision, preferred_element_type=F32
     )
+
+
+def to_squares(flat, squares):
+    rank = squares.shape[-1]
+    for r in range(rank):
+        squares[:, r, :] = flat[:, r * rank : (r + 1) * rank]
+
+
+def to_rows(squares, flat):
+    rank = squares.shape[-1]
+    for r in range(rank):
+        flat[:, r * rank : (r + 1) * rank] = squares[:, r, :]
 
 
 def factor(grams):
@@ -77,12 +91,13 @@
     shape,
     levels,
     basis_ref,
-    child_ref,
-    upper_ref,
+    child_rows,
+    upper_rows,
     vec_ref,
     ortho_ref,
     child_new_ref,
-    top_new_ref,
+    child_out,
+    top_out,
     lower_ref,
     window_ref,
     table_ref,
@@ -90,6 +105,9 @@
     stack_ref,
     term_ref,
     got_ref,
+    child_ref,
+    upper_ref,
+    top_new_ref,
     x_sem,
     send_sem,
     recv_sem,
@@ -243,6 +261,8 @@
             def _():
                 hop_in(stage, side).wait_recv()
 
+    to_squares(child_rows, child_ref)
+    to_squares(upper_rows.at[0], upper_ref)
     pad = jnp.zeros((rank, rank), BF16)
 
     def pack(entry, coeff, lower_t):
@@ -281,8 +301,6 @@
     else:
         for index in range(len(SENDS)):
             direct_copy(index).start()
-    vector_copies[2].start()
-    vector_copies[3].start()
     exchanges = []
     for level in range(levels):
         up = mm(lower_t, upper_ref[level])
@@ -291,16 +309,22 @@
         copy = remote(20 + level, term_ref.at[level], got_ref.at[level], partner(level))
         copy.start()
         exchanges.append(copy)
-        if relay and level in (2, 4):
-            take_hops(level // 2 - 1)
-            start_hops(level // 2)
-            start_rows(level // 2)
+        if relay and level in RELAY_LEVELS:
+            stage = RELAY_LEVELS.index(level)
+            take_hops(stage)
+            start_hops(stage + 1)
+            start_rows(stage + 1)
+        if level == LATE_LEVEL:
+            vector_copies[2].start()
+            vector_copies[3].start()
         copy.wait_recv()
         ((lower_t, inverse),) = factor([term + got_ref[level]])
         top_new_ref[level] = mm(up, inverse, 1, 1)
+    to_rows(child_new_ref, child_out)
+    to_rows(top_new_ref, top_out.at[0])
     if relay:
         for stage in range(cols - 1):
-            if 2 * stage + 2 >= levels:
+            if stage >= len(RELAY_LEVELS):
                 take_hops(stage)
                 if stage + 1 < cols - 1:
                     start_hops(stage + 1)
@@ -341,19 +365,22 @@
     child_ref,
     lower_ref,
     table_ref,
-    coupling_ref,
+    coupling_rows_ref,
     near_rows,
     near_cols,
     near_counts,
     far_rows,
     far_cols,
     far_counts,
-    coupling_new_ref,
+    coupling_out,
     product_ref,
     near_ref,
     far_ref,
     desc_ref,
+    coupling_ref,
+    coupling_new_ref,
 ):
+    to_squares(coupling_rows_ref, coupling_ref)
     me = lax.axis_index("row") * shape[1] + lax.axis_index("col")
     slots, points, _ = blocks_ref.shape
     leaf_count, rank, _ = ortho_ref.shape
@@ -424,6 +451,7 @@
         low = new.astype(BF16)
         term = mm(low, item[:, :nvec], precision=None)
         far_ref[row] = far_ref[row] + term
+    to_rows(coupling_new_ref, coupling_out)
     for l in range(leaf_count):
         desc_ref[l] = (far_ref[l] + mm(child_ref[l], far_ref[leaf_count])).astype(BF16)
     tile = 256
@@ -475,22 +503,26 @@
     def tree(*refs):
         tree_kernel(shape, levels, *refs)
 
-    ortho, child_new, top_new, lowers, window, table = pl.pallas_call(
+    ortho, child_new, child_out, top_out, lowers, window, table = pl.pallas_call(
         tree,
         name="tree",
         out_shape=(
             jax.ShapeDtypeStruct(leaf_basis.shape, F32),
             jax.ShapeDtypeStruct((leaf_count,) + square, F32),
-            jax.ShapeDtypeStruct((levels,) + square, F32),
+            jax.ShapeDtypeStruct(child_transfer.shape, F32),
+            jax.ShapeDtypeStruct(top_transfer.shape, F32),
             jax.ShapeDtypeStruct((leaf_count + 1,) + square, F32),
             jax.ShapeDtypeStruct((2,) + vectors.shape, BF16),
             jax.ShapeDtypeStruct((slots, rank, held), BF16),
         ),
         in_specs=[vmem, vmem, vmem, hbm],
-        out_specs=(vmem, vmem, vmem, vmem, hbm, hbm),
+        out_specs=(vmem, vmem, vmem, vmem, vmem, hbm, hbm),
         scratch_shapes=[
             pltpu.VMEM(vectors.shape, BF16),
             pltpu.VMEM((4, rank, held), BF16),
+            pltpu.VMEM((levels,) + square, F32),
+            pltpu.VMEM((levels,) + square, F32),
+            pltpu.VMEM((leaf_count,) + square, F32),
             pltpu.VMEM((levels,) + square, F32),
             pltpu.VMEM((levels,) + square, F32),
             pltpu.SemaphoreType.DMA,
@@ -498,12 +530,12 @@
             pltpu.SemaphoreType.DMA((copies,)),
         ],
         compiler_params=pltpu.CompilerParams(
-            collective_id=0, has_side_effects=True, vmem_limit_bytes=32 * 1024 * 1024
+            collective_id=0, has_side_effects=True, vmem_limit_bytes=60 * 1024 * 1024
         ),
     )(
         leaf_basis,
-        child_transfer.reshape((leaf_count,) + square),
-        top_transfer.reshape((levels,) + square),
+        child_transfer,
+        top_transfer,
         vectors,
     )
 
@@ -514,7 +546,7 @@
         apply,
         name="apply",
         out_shape=(
-            jax.ShapeDtypeStruct((coupling.shape[0],) + square, F32),
+            jax.ShapeDtypeStruct(coupling.shape, F32),
             jax.ShapeDtypeStruct(vectors.shape, BF16),
         ),
         in_specs=[vmem] * 8 + [smem] * 6,
@@ -523,8 +555,10 @@
             pltpu.VMEM((leaf_count * points, 3 * leaf_count * points), BF16),
             pltpu.VMEM((leaf_count + 1, rank, nvec), F32),
             pltpu.VMEM((leaf_count, rank, nvec), BF16),
+            pltpu.VMEM((coupling.shape[0],) + square, F32),
+            pltpu.VMEM((coupling.shape[0],) + square, F32),
         ],
-        compiler_params=pltpu.CompilerParams(vmem_limit_bytes=48 * 1024 * 1024),
+        compiler_params=pltpu.CompilerParams(vmem_limit_bytes=60 * 1024 * 1024),
     )(
         near_blocks,
         window,
@@ -533,7 +567,7 @@
         child_new,
         lowers,
         table,
-        coupling.reshape((-1,) + square),
+        coupling,
         near_rows,
         near_cols,
         near_counts,
@@ -543,9 +577,9 @@
     )
     return (
         ortho,
-        child_new.reshape(leaf_count, -1),
-        top_new.reshape(1, levels, -1),
-        coupling_new.reshape(coupling.shape),
+        child_out,
+        top_out,
+        coupling_new,
         product,
     )
 

time: 129 us -> 104 us (0.81)
  local copies, waits for them, and re-layouts: 19.2 us -> 3.6 us
  Pallas kernels: 107 us -> 98.8 us
    pallas_call x1, Pallas kernels: 96.1 us -> 85.5 us  [body(): pl.pallas_call(tree, name='tree', out_shape=(jax.ShapeDtypeStruct(leaf_ba...]
    unnamed x33 -> x10, local copies, waits for them, and re-layouts: 11.4 us -> 3.6 us
    reshape x6 -> x0, local copies, waits for them, and re-layouts: 7.79 us -> none  [the longest x1 1.91 us: body(): coupling.reshape((-1,) + square)]
    pallas_call x1, Pallas kernels: 11 us -> 13.2 us  [body(): pl.pallas_call(apply, name='apply', out_shape=(jax.ShapeDtypeStruct(coupl...]
where the time goes in v3:
time: 104 us
  Pallas kernels  98.8 us (95%)
  local copies, waits for them, and re-layouts  3.6 us (3%)
  between operations  1.31 us (1%)
    pallas_call x1, Pallas kernels, body(): pl.pallas_call(tree, name='tree', out_shape=(jax.ShapeDtypeStruct(leaf_ba...  85.5 us
    pallas_call x1, Pallas kernels, body(): pl.pallas_call(apply, name='apply', out_shape=(jax.ShapeDtypeStruct(coupl...  13.2 us
    unnamed x10, local copies, waits for them, and re-layouts  3.6 us

profile of v3, /device:TPU:0, one launch (start us, length us, event | category | flops | bytes accessed | tf_op | source)
XLA Modules:
  0.0 103.7 jit_solution(18045009132214911005)
XLA Ops:
  0.6 1.6 %copy.17.refs_2_ = f32[1,5,4096]{2,1,0:T(8,128)} copy(f32[1,5,4096]{2,0,1:T(1,128)} %param.14) | data formatting | bytes 163840 | tf_op args[2]
  2.2 85.5 %tree.1 = (f32[2,64,256]{2,1,0:T(8,128)}, f32[2,64,64]{2,1,0:T(8,128)}, f32[2,4096]{1,0:T(2,128)}, f32[1,5,4096]{2,1,0:T(8,128)}, f32[3,64,64]{2,1,0:T(8,128)}, ...) custom-call(f32[2,64,256]{2,1,0:T(8,128)} %refs_0_.2, f32[2,4096]{1,0:T(2,128)} %refs_1_.1, ...), custom_call_target="tpu_custom_call" | custom-call | tf_op jit(solution)/shard_map/tree/pallas_call | solution.py:506
  88.4 0.0 copy-start.1
  88.4 0.0 copy-start
  88.4 0.0 copy-start.2
  88.4 13.2 %apply.1 = (f32[15,4096]{1,0:T(8,128)}, bf16[512,1024]{1,0:T(8,128)(2,1)}) custom-call(bf16[10,256,256]{2,1,0:T(8,128)(2,1)} %refs_0_.3, bf16[2,512,1024]{2,1,0:T(8,128)(2,1)} %get-tuple-element.17.refs_1_, bf16[512,1024]{1,0:T(8,128)(2,1)} %refs_2_.2, f32[2,64,256]{2,1,0:T(8,128)} %get-tuple-element.33.refs_3_, f32[2,64,64]{2,1,0:T(8,128)} %get-tuple-element.18.refs_4_, ...), custom_call_target="tpu_custom_call" | custom-call | tf_op jit(solution)/shard_map/apply/pallas_call | solution.py:545
  101.7 0.0 copy-done.1
  101.7 0.7 copy.18
  102.4 0.0 copy-done
  102.4 0.7 copy.22
  103.1 0.0 copy-done.2
  103.1 0.6 copy.23
Async XLA Ops:
  88.4 13.3 %copy-start.1 = (f32[1,5,4096]{2,1,0:T(8,128)S(1)}, f32[1,5,4096]{2,1,0:T(8,128)}, u32[]{:S(2)}) copy-start(f32[1,5,4096]{2,1,0:T(8,128)} %get-tuple-element.25) | copy-start | bytes 245764
  88.4 14.0 %copy-start = (f32[2,64,256]{2,1,0:T(8,128)S(1)}, f32[2,64,256]{2,1,0:T(8,128)}, u32[]{:S(2)}) copy-start(f32[2,64,256]{2,1,0:T(8,128)} %get-tuple-element.33.refs_3_) | copy-start | bytes 393220
  88.4 14.6 %copy-start.2 = (f32[2,4096]{1,0:T(2,128)S(1)}, f32[2,4096]{1,0:T(2,128)}, u32[]{:S(2)}) copy-start(f32[2,4096]{1,0:T(2,128)} %get-tuple-element.34) | copy-start | bytes 98308
